TPU v7x, 32 devices: a whole 2x2x4 slice. The times are simulated.
32 devices in a mesh: groups: 2 (over x), mp: 8 (over z, y), dp: 2 (over core).
Axes of the slice: x: 2, y: 2, z: 4, core: 2. Of those that a mesh axis runs over, the one named last changes fastest.
Arguments:
- latents: bfloat16 [12, 128, 128, 320], P(('groups', 'dp'), 'mp'), parts along dimension 0, may hold values from -6 to 6
- room_labels: int32 [12, 128, 128], P(('groups', 'dp'), 'mp'), parts along dimension 0, may hold values from 0 to 15
- timesteps: int32 [12], P(('groups', 'dp')), parts along dimension 0, may hold values from 0 to 999
- label_table: bfloat16 [16, 320], replicated, may hold values from -6 to 6
- time_weight: bfloat16 [1280, 320], replicated, may hold values from -0.15625 to 0.15625
- trunk_weight: bfloat16 [320, 3, 3, 320], P('mp'), may hold values from -0.109375 to 0.109375
- control_weight: bfloat16 [320, 3, 3, 320], P('mp'), may hold values from -0.109375 to 0.109375
- mix_weight: bfloat16 [320, 320], P('mp'), may hold values from -0.3125 to 0.3125
- cotangent: bfloat16 [12, 128, 128, 320], P(('groups', 'dp'), 'mp'), parts along dimension 0, may hold values from -0.08984375 to 0.08984375
Outputs:
- output: bfloat16 [12, 128, 128, 320], P(('groups', 'dp'), 'mp'), parts along dimension 0
- grad_control: float32 [640, 3, 3, 320], P(('groups', 'mp')), parts along dimension 0
- grad_mix: float32 [640, 320], P(('groups', 'mp')), parts along dimension 0
- grad_table: float32 [32, 320], P('groups'), parts along dimension 0
There are 2 independent parts, one for each index of `groups`. A program takes and returns all parts, laid end to end along the dimension named above; an argument that names none is the same for every part. Nothing has to cross between parts.
All inputs are finite; a program needn't handle non-finite values.
Results may differ from a plain program's by a relative error of at most 0.0057.
Values may be sent and summed in bfloat16 or wider, within the bound.
A program may use at most 256 MiB of HBM per device.

v0:
```python
import math

import jax
import jax.numpy as jnp
from jax import lax
from jax.sharding import PartitionSpec as P


def with_halo(cells, sides, width):
    for axis, dim in sides:
        count = lax.axis_size(axis)
        ends = count - 1
        head = lax.slice_in_dim(cells, 0, width, axis=dim)
        tail = lax.slice_in_dim(cells, cells.shape[dim] - width, cells.shape[dim], axis=dim)
        cells = jnp.concatenate(
            [
                lax.ppermute(tail, axis, [(i, (i + 1) % count) for i in range(ends)]),
                cells,
                lax.ppermute(head, axis, [((i + 1) % count, i) for i in range(ends)]),
            ],
            axis=dim,
        )
    return cells


def sinusoid(timesteps, embed_width):
    half_width = embed_width // 2
    indices = jnp.arange(half_width, dtype=jnp.float32)
    frequency = jnp.exp(-math.log(10000.0) * indices / half_width)
    angles = timesteps.astype(jnp.float32)[:, None] * frequency[None, :]
    return jnp.concatenate([jnp.cos(angles), jnp.sin(angles)], axis=1)


def forward_taps(frame, kernel):
    row_count = frame.shape[1] - 2
    span_cols = frame.shape[2] - 2
    running = jnp.zeros(frame.shape[:1] + (row_count, span_cols, kernel.shape[3]), jnp.float32)
    for tap_row in range(3):
        for tap_col in range(3):
            running = running + jnp.einsum(
                "bhwc,cd->bhwd",
                frame[:, tap_row : tap_row + row_count, tap_col : tap_col + span_cols],
                kernel[:, tap_row, tap_col],
                preferred_element_type=jnp.float32,
            )
    return running


def backward_taps(frame, kernel):
    row_count = frame.shape[1] - 2
    span_cols = frame.shape[2] - 2
    running = jnp.zeros(frame.shape[:1] + (row_count, span_cols, kernel.shape[0]), jnp.float32)
    for tap_row in range(3):
        for tap_col in range(3):
            running = running + jnp.einsum(
                "bhwd,cd->bhwc",
                frame[
                    :, 2 - tap_row : 2 - tap_row + row_count, 2 - tap_col : 2 - tap_col + span_cols
                ],
                kernel[:, tap_row, tap_col],
                preferred_element_type=jnp.float32,
            )
    return running


def per_device(
    latents,
    room_labels,
    timesteps,
    label_table,
    time_weight,
    trunk_weight,
    control_weight,
    mix_weight,
    cotangent,
):
    images, row_count, span_cols, channels = latents.shape
    rooms = label_table.shape[0]
    onehot = (room_labels[..., None] == jnp.arange(rooms, dtype=jnp.int32)).astype(jnp.bfloat16)
    embedded = jnp.einsum("bhwr,rc->bhwc", onehot, label_table, preferred_element_type=jnp.float32)
    control_in = (latents.astype(jnp.float32) + embedded).astype(jnp.bfloat16)
    stacked = jnp.stack([latents, control_in])
    framed = with_halo(stacked, (("mp", 2),), 1)
    framed = jnp.pad(framed, ((0, 0), (0, 0), (0, 0), (1, 1), (0, 0)))
    trunk_frame = framed[0]
    control_frame = framed[1]
    time_features = jax.nn.silu(sinusoid(timesteps, time_weight.shape[0])).astype(jnp.bfloat16)
    time_shift = jnp.dot(time_features, time_weight, preferred_element_type=jnp.float32)[
        :, None, None, :
    ]
    trunk_full = lax.all_gather(trunk_weight, "mp", axis=0, tiled=True)
    trunk_pre = forward_taps(trunk_frame, trunk_full) + time_shift
    control_full, mix_full = (
        lax.all_gather(control_weight, "mp", axis=0, tiled=True),
        lax.all_gather(mix_weight, "mp", axis=0, tiled=True),
    )
    control_pre = forward_taps(control_frame, control_full) + time_shift
    gated_act = jax.nn.silu(control_pre).astype(jnp.bfloat16)
    mixed_out = jnp.einsum("bhwc,cd->bhwd", gated_act, mix_full, preferred_element_type=jnp.float32)
    output = (jax.nn.silu(trunk_pre) + mixed_out).astype(jnp.bfloat16)
    back_gate = jnp.einsum("bhwd,cd->bhwc", cotangent, mix_full, preferred_element_type=jnp.float32)
    sigmoid_val = jax.nn.sigmoid(control_pre)
    back_pre = (back_gate * sigmoid_val * (1.0 + control_pre * (1.0 - sigmoid_val))).astype(
        jnp.bfloat16
    )
    back_frame = with_halo(back_pre, (("mp", 1),), 1)
    back_frame = jnp.pad(back_frame, ((0, 0), (0, 0), (1, 1), (0, 0)))
    back_kernel = lax.all_gather(control_weight, "mp", axis=0, tiled=True)
    back_in = backward_taps(back_frame, back_kernel)
    table_local = jnp.einsum(
        "bhwr,bhwc->rc", onehot.astype(jnp.float32), back_in, precision=lax.Precision.HIGHEST
    )
    grad_table = lax.psum(table_local, ("mp", "dp"))
    pieces = []
    for tap_row in range(3):
        for tap_col in range(3):
            pieces.append(
                jnp.einsum(
                    "bhwc,bhwd->cd",
                    control_frame[:, tap_row : tap_row + row_count, tap_col : tap_col + span_cols],
                    back_pre,
                    preferred_element_type=jnp.float32,
                )
            )
    kernel_rows = jnp.stack(pieces, axis=1).reshape(channels, 9 * channels)
    mix_rows = jnp.einsum("bhwc,bhwd->cd", gated_act, cotangent, preferred_element_type=jnp.float32)
    grad_term = jnp.concatenate([kernel_rows, mix_rows], axis=1)
    grad_rows = lax.psum_scatter(grad_term, "mp", scatter_dimension=0, tiled=True)
    grad_rows = lax.psum(grad_rows, "dp")
    grad_control = grad_rows[:, : 9 * channels].reshape(grad_rows.shape[0], 3, 3, channels)
    grad_mix = grad_rows[:, 9 * channels :]
    return (output, grad_control, grad_mix, grad_table)


def solution(mesh):
    in_specs = (
        P(("groups", "dp"), "mp", None, None),
        P(("groups", "dp"), "mp", None),
        P(("groups", "dp")),
        P(),
        P(),
        P("mp", None, None, None),
        P("mp", None, None, None),
        P("mp", None),
        P(("groups", "dp"), "mp", None, None),
    )
    out_specs = (
        P(("groups", "dp"), "mp", None, None),
        P(("groups", "mp"), None, None, None),
        P(("groups", "mp"), None),
        P("groups", None),
    )
    return jax.shard_map(
        per_device, mesh=mesh, in_specs=in_specs, out_specs=out_specs, check_vma=False
    )
```

profile of v0, /device:TPU:0, one launch (start us, length us, event | category | flops | bytes accessed | tf_op | source)
XLA Modules:
  0.0 457.2 jit_solution(16254729280796380880)
XLA Ops:
  19.7 49.6 %all_gather.12 = bf16[320,320]{1,0:T(8,128)(2,1)S(1)} all-gather(bf16[40,320]{1,0:T(8,128)(2,1)S(1)} %copy-done.13), channel_id=1, replica_groups=mesh['groups'=2,'mp'=8,'dp'=2] {'mp'}, dimensions={0}, use_global_device_ids=true | all-gather | bytes 230400 | tf_op jit(solution)/shard_map/all_gather | solution.py:95
  69.9 18.2 %select_maximum_fusion = bf16[2,3,18,130,320]{3,4,2,1,0:T(8,128)(2,1)S(1)} fusion(bf16[2,3,1,128,320]{3,4,2,1,0:T(8,128)(2,1)S(1)} %collective-permute-done.1, bf16[2,3,1,128,320]{3,4,2,1,0:T(8,128)(2,1)S(1)} %collective-permute-done, bf16[1,3,16,128,320]{3,4,2,1,0:T(8,128)(2,1)} %copy-done.6, bf16[1,3,16,128,320]{3,4,2,1,0:T(8,128)(2,1)} %bitcast.302), kind=kLoop, calls=%fused_computation.5 | loop fusion | flops 67392000 | bytes 17832960 | tf_op jit(solution)/shard_map/concatenate | solution.py:15
  88.1 7.0 %slice_bitcast_fusion.1 = (bf16[3,18,130,320]{2,3,1,0:T(8,128)(2,1)}, bf16[3,18,130,320]{2,3,1,0:T(8,128)(2,1)}) fusion(bf16[2,3,18,130,320]{3,4,2,1,0:T(8,128)(2,1)S(1)} %select_maximum_fusion), kind=kLoop, calls=%fused_computation.17 | loop fusion | bytes 17971200 | tf_op jit(solution)/shard_map/squeeze | solution.py:85
  95.1 9.1 %fusion.64 = f32[3,16,128,320]{2,3,1,0:T(8,128)} fusion(bf16[3,18,130,320]{2,3,1,0:T(8,128)(2,1)} %get-tuple-element.13, bf16[320,3,3,320]{3,0,2,1:T(8,128)(2,1)} %all-gather.5.cloned.1.call-done), kind=kOutput, calls=%fused_computation.79 | convolution fusion | flops 1258291200 | bytes 12042240 | tf_op jit(solution)/shard_map/bhwc,cd->bhwd/dot_general | solution.py:40
  115.0 5.5 %fusion.76 = f32[3,16,128,320]{2,3,1,0:T(8,128)} fusion(bf16[3,18,130,320]{2,3,1,0:T(8,128)(2,1)S(1)} %copy-done.2, bf16[320,3,3,320]{3,0,2,1:T(8,128)(2,1)S(1)} %copy-done.9), kind=kOutput, calls=%fused_computation.91 | convolution fusion | flops 1258291200 | bytes 12042240 | tf_op jit(solution)/shard_map/bhwc,cd->bhwd/dot_general | solution.py:40
  125.8 5.8 %fusion.84 = f32[3,16,128,320]{2,3,1,0:T(8,128)} fusion(bf16[3,18,130,320]{2,3,1,0:T(8,128)(2,1)S(1)} %copy-done.2, bf16[320,3,3,320]{3,0,2,1:T(8,128)(2,1)S(1)} %copy-done.9), kind=kOutput, calls=%fused_computation.99 | convolution fusion | flops 1258291200 | bytes 12042240 | tf_op jit(solution)/shard_map/bhwc,cd->bhwd/dot_general | solution.py:40
  131.7 5.7 %fusion.88 = f32[3,16,128,320]{2,3,1,0:T(8,128)} fusion(bf16[3,18,130,320]{2,3,1,0:T(8,128)(2,1)S(1)} %copy-done.2, bf16[320,3,3,320]{3,0,2,1:T(8,128)(2,1)S(1)} %copy-done.9), kind=kOutput, calls=%fused_computation.103 | convolution fusion | flops 1258291200 | bytes 12042240 | tf_op jit(solution)/shard_map/bhwc,cd->bhwd/dot_general | solution.py:40
  142.7 28.2 %multiply_convert_fusion.1 = (bf16[3,16,128,320]{2,3,1,0:T(8,128)(2,1)}, f32[3,16,128,320]{2,3,1,0:T(8,128)}) fusion(f32[3,320]{1,0:T(4,128)S(1)} %fusion.163, bf16[3,18,130,320]{2,3,1,0:T(8,128)(2,1)} %get-tuple-element.13, bf16[320,3,3,320]{3,0,2,1:T(8,128)(2,1)S(1)} %copy-done.9, f32[3,16,128,320]{2,3,1,0:T(8,128)} %fusion.64, ...), kind=kOutput, calls=%fused_computation.29 | convolution fusion | flops 1285816320 | bytes 78895104 | tf_op jit(solution)/shard_map/bhwc,cd->bhwd/dot_general | solution.py:40
  171.0 7.3 %multiply_convert_fusion = bf16[3,16,128,320]{2,3,1,0:T(8,128)(2,1)S(1)} fusion(f32[3,16,128,320]{2,3,1,0:T(8,128)} %get-tuple-element.21, bf16[3,16,128,320]{2,3,1,0:T(8,128)(2,1)} %param.17, bf16[320,320]{1,0:T(8,128)(2,1)S(1)} %all_gather.12), kind=kOutput, calls=%fused_computation.27 | convolution fusion | flops 1275985920 | bytes 15933440 | tf_op jit(solution)/shard_map/bhwd,cd->bhwc/dot_general | solution.py:101
  178.3 5.7 %fusion.101 = f32[320,9,320]{0,2,1:T(8,128)S(1)} fusion(bf16[3,16,128,320]{2,3,1,0:T(8,128)(2,1)S(1)} %multiply_convert_fusion, bf16[3,18,130,320]{2,3,1,0:T(8,128)(2,1)} %get-tuple-element.13), kind=kOutput, calls=%fused_computation.110 | convolution fusion | flops 1258291200 | bytes 8355840 | tf_op jit(solution)/shard_map/bhwc,bhwd->cd/dot_general | solution.py:118
  211.0 5.6 %copy.38 = f32[320,2880]{1,0:T(8,128)} copy(f32[320,2880]{0,1:T(8,128)} %bitcast.304) | data formatting | bytes 7372800 | tf_op jit(solution)/shard_map/reshape | solution.py:125
  216.6 7.6 %fusion.156 = f32[3,16,128,320]{2,3,1,0:T(8,128)} fusion(bf16[3,16,128,320]{2,3,1,0:T(8,128)(2,1)} %get-tuple-element.20, bf16[320,320]{1,0:T(8,128)(2,1)S(1)} %all_gather.12), kind=kOutput, calls=%fused_computation.151 | convolution fusion | flops 1258291200 | bytes 12001280 | tf_op jit(solution)/shard_map/bhwc,cd->bhwd/dot_general | solution.py:99
  228.9 9.0 %fusion.42 = f32[3,16,128,320]{2,3,1,0:T(8,128)} fusion(bf16[3,18,130,320]{2,3,1,0:T(8,128)(2,1)} %get-tuple-element.12, bf16[320,3,3,320]{3,0,2,1:T(8,128)(2,1)} %all-gather.3.cloned.1.call-done), kind=kOutput, calls=%fused_computation.57 | convolution fusion | flops 1258291200 | bytes 12042240 | tf_op jit(solution)/shard_map/bhwc,cd->bhwd/dot_general | solution.py:40
  237.9 7.5 %fusion.44 = f32[3,16,128,320]{2,3,1,0:T(8,128)} fusion(bf16[3,18,130,320]{2,3,1,0:T(8,128)(2,1)} %get-tuple-element.12, bf16[320,3,3,320]{3,0,2,1:T(8,128)(2,1)S(1)} %copy-done.11), kind=kOutput, calls=%fused_computation.59 | convolution fusion | flops 1258291200 | bytes 12042240 | tf_op jit(solution)/shard_map/bhwc,cd->bhwd/dot_general | solution.py:40
  251.0 5.6 %fusion.48 = f32[3,16,128,320]{2,3,1,0:T(8,128)} fusion(bf16[3,18,130,320]{2,3,1,0:T(8,128)(2,1)S(1)} %bitcast.299, bf16[320,3,3,320]{3,0,2,1:T(8,128)(2,1)S(1)} %copy-done.11), kind=kOutput, calls=%fused_computation.63 | convolution fusion | flops 1258291200 | bytes 12042240 | tf_op jit(solution)/shard_map/bhwc,cd->bhwd/dot_general | solution.py:40
  261.8 6.0 %fusion.52 = f32[3,16,128,320]{2,3,1,0:T(8,128)} fusion(bf16[3,18,130,320]{2,3,1,0:T(8,128)(2,1)S(1)} %bitcast.299, bf16[320,3,3,320]{3,0,2,1:T(8,128)(2,1)S(1)} %copy-done.11), kind=kOutput, calls=%fused_computation.67 | convolution fusion | flops 1258291200 | bytes 12042240 | tf_op jit(solution)/shard_map/bhwc,cd->bhwd/dot_general | solution.py:40
  267.9 5.6 %fusion.54 = f32[3,16,128,320]{2,3,1,0:T(8,128)} fusion(bf16[3,18,130,320]{2,3,1,0:T(8,128)(2,1)S(1)} %bitcast.299, bf16[320,3,3,320]{3,0,2,1:T(8,128)(2,1)S(1)} %copy-done.11), kind=kOutput, calls=%fused_computation.69 | convolution fusion | flops 1258291200 | bytes 12042240 | tf_op jit(solution)/shard_map/bhwc,cd->bhwd/dot_general | solution.py:40
  278.8 28.7 %add_convert_fusion = bf16[3,16,128,320]{2,3,1,0:T(8,128)(2,1)} fusion(f32[3,16,128,320]{2,3,1,0:T(8,128)} %fusion.156, f32[3,16,128,320]{2,3,1,0:T(8,128)} %fusion.42, f32[3,16,128,320]{2,3,1,0:T(8,128)} %fusion.44, f32[3,16,128,320]{2,3,1,0:T(8,128)} %fusion.46, f32[3,16,128,320]{2,3,1,0:T(8,128)} %fusion.48, f32[3,16,128,320]{2,3,1,0:T(8,128)} %fusion.50, ...), kind=kOutput, calls=%fused_computation.28 | convolution fusion | flops 1287782400 | bytes 78892800 | tf_op jit(solution)/shard_map/bhwc,cd->bhwd/dot_general | solution.py:40
  307.4 7.6 %fusion.158 = f32[3,16,128,320]{2,3,1,0:T(8,128)} fusion(bf16[3,16,128,320]{2,3,1,0:T(8,128)(2,1)} %copy-done.3, bf16[320,3,3,320]{3,0,2,1:T(8,128)(2,1)S(1)} %copy-done.9), kind=kOutput, calls=%fused_computation.153 | convolution fusion | flops 1258291200 | bytes 12042240 | tf_op jit(solution)/shard_map/bhwd,cd->bhwc/dot_general | solution.py:55
  325.7 6.3 %fusion.9 = bf16[3,18,130,320]{2,3,1,0:T(8,128)(2,1)S(1)} fusion(bf16[3,1,128,320]{2,3,1,0:T(8,128)(2,1)S(1)} %collective-permute-done.3, bf16[3,16,128,320]{2,3,1,0:T(8,128)(2,1)S(1)} %copy-done.4, bf16[3,1,128,320]{2,3,1,0:T(8,128)(2,1)S(1)} %collective-permute-done.2), kind=kLoop, calls=%fused_computation.15 | loop fusion | flops 26956800 | bytes 8916480 | tf_op jit(solution)/shard_map/concatenate | solution.py:15
  332.0 5.6 %fusion.30 = f32[3,16,128,320]{2,3,1,0:T(8,128)} fusion(bf16[3,18,130,320]{2,3,1,0:T(8,128)(2,1)S(1)} %fusion.9, bf16[320,3,3,320]{3,0,2,1:T(8,128)(2,1)S(1)} %copy-done.9), kind=kOutput, calls=%fused_computation.45 | convolution fusion | flops 1258291200 | bytes 12042240 | tf_op jit(solution)/shard_map/bhwd,cd->bhwc/dot_general | solution.py:55
  342.9 5.5 %fusion.34 = f32[3,16,128,320]{2,3,1,0:T(8,128)} fusion(bf16[3,18,130,320]{2,3,1,0:T(8,128)(2,1)S(1)} %fusion.9, bf16[320,3,3,320]{3,0,2,1:T(8,128)(2,1)S(1)} %copy-done.9), kind=kOutput, calls=%fused_computation.49 | convolution fusion | flops 1258291200 | bytes 12042240 | tf_op jit(solution)/shard_map/bhwd,cd->bhwc/dot_general | solution.py:55
  364.7 24.3 %fusion.152 = f32[16,320]{1,0:T(8,128)S(1)} fusion(f32[3,16,128,320]{2,3,1,0:T(8,128)} %fusion.28, f32[3,16,128,320]{2,3,1,0:T(8,128)} %fusion.23, f32[3,16,128,320]{2,3,1,0:T(8,128)} %fusion.30, f32[3,16,128,320]{2,3,1,0:T(8,128)} %fusion.32, f32[3,16,128,320]{2,3,1,0:T(8,128)} %fusion.158, f32[3,16,128,320]{2,3,1,0:T(8,128)} %fusion.34, ...), kind=kOutput, calls=%fused_computation.128 | convolution fusion | flops 393314304 | bytes 70823936 | tf_op jit(solution)/shard_map/bhwr,bhwc->rc/dot_general | solution.py:110
  389.0 57.6 %psum.15 = f32[16,320]{1,0:T(8,128)} all-reduce(f32[16,320]{1,0:T(8,128)S(1)} %fusion.152), channel_id=1, replica_groups=mesh['groups'=2,'mp'=8,'dp'=2] {'mp','dp'}, use_global_device_ids=true, to_apply=%region_2.3 | all-reduce | flops 5120 | bytes 40960 | tf_op jit(solution)/shard_map/psum | solution.py:113
  (100 shorter events, 118.2 us)
Async XLA Ops:
  7.2 62.4 %copy-start = (bf16[1280,320]{0,1:T(8,128)(2,1)S(1)}, bf16[1280,320]{0,1:T(8,128)(2,1)}, u32[]{:S(2)}) copy-start(bf16[1280,320]{0,1:T(8,128)(2,1)} %param.13) | copy-start | bytes 2457604
  7.2 87.9 %all-gather.5.cloned.1.call-start = ((), (), s32[]{:S(2)}) async-start(), calls=%async_computation.2 | async-start | bytes 2488320 | tf_op jit(solution)/shard_map/all_gather | solution.py:94
  7.9 11.8 %copy-start.13 = (bf16[40,320]{1,0:T(8,128)(2,1)S(1)}, bf16[40,320]{1,0:T(8,128)(2,1)}, u32[]{:S(2)}) copy-start(bf16[40,320]{1,0:T(8,128)(2,1)} %param.16) | copy-start | bytes 76804
  7.9 61.5 %copy-start.15 = (s32[3]{0:T(128)S(1)}, s32[3]{0:T(128)}, u32[]{:S(2)}) copy-start(s32[3]{0:T(128)} %param.11) | copy-start | bytes 40
  7.9 220.9 %all-gather.3.cloned.1.call-start = ((), (), s32[]{:S(2)}) async-start(), calls=%async_computation.1 | async-start | bytes 2488320 | tf_op jit(solution)/shard_map/all_gather | solution.py:91
  13.4 56.4 %collective-permute-start = (bf16[2,3,1,128,320]{3,4,2,1,0:T(8,128)(2,1)S(1)}, bf16[2,3,1,128,320]{3,4,2,1,0:T(8,128)(2,1)S(1)}, u32[]{:S(2)}, u32[]{:S(2)}) collective-permute-start(bf16[2,3,1,128,320]{3,4,2,1,0:T(8,128)(2,1)S(1)} %get-tuple-element.14), channel_id=1, source_target_pairs={{0,2},{2,4},{4,6},{6,8},{8,10},{10,12},{12,14},{1,3},{3,5},{5,7},{... | collective-permute-start | bytes 1474568 | tf_op jit(solution)/shard_map/ppermute | solution.py:17
  18.3 51.5 %collective-permute-start.1 = (bf16[2,3,1,128,320]{3,4,2,1,0:T(8,128)(2,1)S(1)}, bf16[2,3,1,128,320]{3,4,2,1,0:T(8,128)(2,1)S(1)}, u32[]{:S(2)}, u32[]{:S(2)}) collective-permute-start(bf16[2,3,1,128,320]{3,4,2,1,0:T(8,128)(2,1)S(1)} %get-tuple-element.15), channel_id=1, source_target_pairs={{2,0},{4,2},{6,4},{8,6},{10,8},{12,10},{14,12},{3,1},{5,3},{7,5},{... | collective-permute-start | bytes 1474568 | tf_op jit(solution)/shard_map/ppermute | solution.py:19
  19.7 345.0 %reduce-scatter.4.cloned.1.call-start = ((), (), s32[]{:S(2)}) async-start(), calls=%async_computation.4 | async-start | bytes 4608000
  95.1 9.1 %copy-start.2 = (bf16[3,18,130,320]{2,3,1,0:T(8,128)(2,1)S(1)}, bf16[3,18,130,320]{2,3,1,0:T(8,128)(2,1)}, u32[]{:S(2)}) copy-start(bf16[3,18,130,320]{2,3,1,0:T(8,128)(2,1)} %get-tuple-element.13) | copy-start | bytes 13478404
  95.1 9.1 %copy-start.9 = (bf16[320,3,3,320]{3,0,2,1:T(8,128)(2,1)S(1)}, bf16[320,3,3,320]{3,0,2,1:T(8,128)(2,1)}, u32[]{:S(2)}) copy-start(bf16[320,3,3,320]{3,0,2,1:T(8,128)(2,1)} %all-gather.5.cloned.1.call-done) | copy-start | bytes 5529604
  178.3 28.3 %copy-start.3 = (bf16[3,16,128,320]{2,3,1,0:T(8,128)(2,1)}, bf16[3,16,128,320]{2,3,1,0:T(8,128)(2,1)S(1)}, u32[]{:S(2)}) copy-start(bf16[3,16,128,320]{2,3,1,0:T(8,128)(2,1)S(1)} %multiply_convert_fusion) | copy-start | bytes 11796484
  178.3 14.4 %slice-start.3 = ((s8[8847360]{0:T(1024)(128)(4,1)}), s8[4194304]{0:T(1024)(128)(4,1)S(1)}, s32[]{:S(2)}) async-start(s8[8847360]{0:T(1024)(128)(4,1)} %bitcast.300), calls=%async_computation.8 | async-start | bytes 8388608
  178.3 14.4 %slice-start.4 = ((s8[8847360]{0:T(1024)(128)(4,1)}), s8[4194304]{0:T(1024)(128)(4,1)S(1)}, s32[]{:S(2)}) async-start(s8[8847360]{0:T(1024)(128)(4,1)} %bitcast.300), calls=%async_computation.9 | async-start | bytes 8388608
  184.1 136.3 %collective-permute-start.2 = (bf16[3,1,128,320]{2,3,1,0:T(8,128)(2,1)S(1)}, bf16[3,1,128,320]{2,3,1,0:T(8,128)(2,1)S(1)}, u32[]{:S(2)}, u32[]{:S(2)}) collective-permute-start(bf16[3,1,128,320]{2,3,1,0:T(8,128)(2,1)S(1)} %get-tuple-element.16), channel_id=1, source_target_pairs={{0,2},{2,4},{4,6},{6,8},{8,10},{10,12},{12,14},{1,3},{3,5},{5,7},{... | collective-permute-start | bytes 737288 | tf_op jit(solution)/shard_map/ppermute | solution.py:17
  185.4 129.6 %collective-permute-start.3 = (bf16[3,1,128,320]{2,3,1,0:T(8,128)(2,1)S(1)}, bf16[3,1,128,320]{2,3,1,0:T(8,128)(2,1)S(1)}, u32[]{:S(2)}, u32[]{:S(2)}) collective-permute-start(bf16[3,1,128,320]{2,3,1,0:T(8,128)(2,1)S(1)} %get-tuple-element.17), channel_id=1, source_target_pairs={{2,0},{4,2},{6,4},{8,6},{10,8},{12,10},{14,12},{3,1},{5,3},{7,5},{... | collective-permute-start | bytes 737288 | tf_op jit(solution)/shard_map/ppermute | solution.py:19
  216.6 7.6 %copy-start.7 = (bf16[3,16,128,320]{2,3,1,0:T(8,128)(2,1)S(1)}, bf16[3,16,128,320]{2,3,1,0:T(8,128)(2,1)}, u32[]{:S(2)}) copy-start(bf16[3,16,128,320]{2,3,1,0:T(8,128)(2,1)} %get-tuple-element.20) | copy-start | bytes 11796484
  216.6 7.6 %copy-start.14 = (bf16[3,16,128,320]{2,3,1,0:T(8,128)(2,1)S(1)}, bf16[3,16,128,320]{2,3,1,0:T(8,128)(2,1)}, u32[]{:S(2)}) copy-start(bf16[3,16,128,320]{2,3,1,0:T(8,128)(2,1)} %param.17) | copy-start | bytes 11796484
  228.8 217.8 %all-reduce.5.cloned.1.call-start = ((), (), s32[]{:S(2)}) async-start(), calls=%async_computation.3 | async-start | bytes 1024000 | tf_op jit(solution)/shard_map/psum | solution.py:129
  228.9 9.0 %copy-start.11 = (bf16[320,3,3,320]{3,0,2,1:T(8,128)(2,1)S(1)}, bf16[320,3,3,320]{3,0,2,1:T(8,128)(2,1)}, u32[]{:S(2)}) copy-start(bf16[320,3,3,320]{3,0,2,1:T(8,128)(2,1)} %all-gather.3.cloned.1.call-done) | copy-start | bytes 5529604
  228.9 16.5 %slice-start = ((s8[8847360]{0:T(1024)(128)(4,1)}), s8[4194304]{0:T(1024)(128)(4,1)S(1)}, s32[]{:S(2)}) async-start(s8[8847360]{0:T(1024)(128)(4,1)} %bitcast.298), calls=%async_computation.5 | async-start | bytes 8388608
  228.9 16.5 %slice-start.1 = ((s8[8847360]{0:T(1024)(128)(4,1)}), s8[4194304]{0:T(1024)(128)(4,1)S(1)}, s32[]{:S(2)}) async-start(s8[8847360]{0:T(1024)(128)(4,1)} %bitcast.298), calls=%async_computation.6 | async-start | bytes 8388608
  237.9 7.5 %slice-start.2 = ((s8[8847360]{0:T(1024)(128)(4,1)}), s8[458752]{0:T(1024)(128)(4,1)S(1)}, s32[]{:S(2)}) async-start(s8[8847360]{0:T(1024)(128)(4,1)} %bitcast.298), calls=%async_computation.7 | async-start | bytes 917504
  307.4 7.6 %copy-start.4 = (bf16[3,16,128,320]{2,3,1,0:T(8,128)(2,1)S(1)}, bf16[3,16,128,320]{2,3,1,0:T(8,128)(2,1)}, u32[]{:S(2)}) copy-start(bf16[3,16,128,320]{2,3,1,0:T(8,128)(2,1)} %copy-done.3) | copy-start | bytes 11796484
  364.7 85.8 %copy-start.1 = (bf16[1280,320]{0,1:T(8,128)(2,1)S(1)}, bf16[1280,320]{0,1:T(8,128)(2,1)}, u32[]{:S(2)}) copy-start(bf16[1280,320]{0,1:T(8,128)(2,1)} %param.13) | copy-start | bytes 2457604
  (6 other events, 22.6 us)
Sparse Core Ops, SparseCore 0:
  10.2 66.9 all-gather.4
  79.4 49.2 all-gather.2
  228.9 86.5 reduce-scatter.3
  364.8 19.9 all-reduce.4
where the time goes:
time: 461 us; the launch traced here: 457 us
  matrix products  278 us (60%)
  blocking collectives  107 us (23%)
  other arithmetic  27.1 us (6%)
  local copies, waits for them, and re-layouts  20.5 us (4%)
  between operations  14.4 us (3%)
  starting transfers between devices  9.47 us (2%)
    dot_general x18, matrix products, forward_taps(): jnp.einsum('bhwc,cd->bhwd', frame[:, tap_row:tap_row + row_count, tap_col...  154 us
    psum x1, blocking collectives, per_device(): grad_table = lax.psum(table_local, ('mp', 'dp'))  57.6 us
    dot_general x9, matrix products, backward_taps(): jnp.einsum('bhwd,cd->bhwc', frame[:, 2 - tap_row:2 - tap_row + row_count,...  50.8 us
    all_gather x1, blocking collectives, per_device(): lax.all_gather(mix_weight, 'mp', axis=0, tiled=True)  49.6 us
    dot_general x9, matrix products, per_device(): jnp.einsum('bhwc,bhwd->cd', control_frame[:, tap_row:tap_row + row_count,...  27.2 us
    concatenate x2, other arithmetic, with_halo(): jnp.concatenate([lax.ppermute(tail, axis, [(i, (i + 1) % count) for i in...  24.5 us
    dot_general x1, matrix products, per_device(): jnp.einsum('bhwr,bhwc->rc', onehot.astype(jnp.float32), back_in, precisio...  24.3 us
  transfers between devices with their start and end apart: 8, of which 0 were waited for; matrix products, arithmetic and copies ran while one was open for 69% of the time, Pallas kernels for 0%

commit v1 on v0

v1 whole, which is shorter than its diff:
```python
import functools
import math

import jax
import jax.numpy as jnp
from jax import lax
from jax.experimental import pallas as pl
from jax.experimental.pallas import tpu as pltpu
from jax.sharding import PartitionSpec as P

MESH = pl.DeviceIdType.MESH
LANES = 128
MIB = 1024 * 1024


def ring_position(index, count):
    if count != 8:
        return index
    short, long = index % 2, index // 2
    return (1 - short) * long + short * (count - 1 - long)


def ring_index(position, count):
    if count != 8:
        return position
    short = position // (count // 2)
    long = (1 - short) * position + short * (count - 1 - position)
    return 2 * long + short


def signal_all(targets):
    barrier = pltpu.get_barrier_semaphore()
    for target in targets:
        pl.semaphore_signal(barrier, inc=1, device_id=target, device_id_type=MESH)
    pl.semaphore_wait(barrier, len(targets))


def gather_kernel(n, w_ref, f_ref, g_ref, halo_ref, ring_send, ring_recv, sib_send, sib_recv, halo_send, halo_recv, own_sem):
    me = lax.axis_index("mp")
    core = lax.axis_index("dp")
    pos = ring_position(me, n)
    right = {"mp": ring_index((pos + 1) % n, n)}
    left = {"mp": ring_index((pos + n - 1) % n, n)}
    up = {"mp": (me + n - 1) % n}
    down = {"mp": (me + 1) % n}
    sibling = {"dp": 1 - core}
    signal_all((right, left, up, down, sibling))
    half = w_ref.shape[0] // 2
    mine = pl.ds(core * half, half)
    rows = f_ref.shape[1]

    def remote(src, dst, send, recv, target):
        return pltpu.make_async_remote_copy(
            src_ref=src, dst_ref=dst, send_sem=send, recv_sem=recv, device_id=target, device_id_type=MESH
        )

    right_steps = n // 2
    left_steps = n - 1 - right_steps
    pending = []
    ring = {}

    def send(side, step):
        shift = n - step if side == 0 else step
        origin = ring_index((pos + shift) % n, n)
        src = w_ref.at[mine] if step == 0 else g_ref.at[origin, mine]
        slot = side * right_steps + step
        copy = remote(src, g_ref.at[origin, mine], ring_send.at[slot], ring_recv.at[slot], (right, left)[side])
        copy.start()
        ring[side, step] = copy

    send(0, 0)
    if left_steps:
        send(1, 0)
    halo_down = remote(f_ref.at[:, rows - 1], halo_ref.at[0], halo_send.at[0], halo_recv.at[0], down)
    halo_up = remote(f_ref.at[:, 0], halo_ref.at[1], halo_send.at[1], halo_recv.at[1], up)
    halo_down.start()
    halo_up.start()
    own = pltpu.make_async_copy(w_ref, g_ref.at[me], own_sem)
    own.start()
    for step in range(right_steps):
        for side, steps in ((0, right_steps), (1, left_steps)):
            if step >= steps:
                continue
            ring[side, step].wait_recv()
            if step + 1 < steps:
                send(side, step + 1)
            shift = n - step - 1 if side == 0 else step + 1
            origin = ring_index((pos + shift) % n, n)
            slot = side * right_steps + step
            copy = remote(
                g_ref.at[origin, mine], g_ref.at[origin, mine], sib_send.at[slot], sib_recv.at[slot], sibling
            )
            copy.start()
            pending.append(copy)
    for copy in ring.values():
        copy.wait_send()
    for copy in pending:
        copy.wait()
    halo_down.wait()
    halo_up.wait()
    own.wait()


def gather(n, w, f):
    images, _, cols, lanes = f.shape
    return pl.pallas_call(
        functools.partial(gather_kernel, n),
        out_shape=(
            jax.ShapeDtypeStruct((n,) + w.shape, w.dtype),
            jax.ShapeDtypeStruct((2, images, cols, lanes), f.dtype),
        ),
        in_specs=[pl.BlockSpec(memory_space=pl.ANY)] * 2,
        out_specs=(pl.BlockSpec(memory_space=pl.ANY),) * 2,
        scratch_shapes=[
            pltpu.SemaphoreType.DMA((n,)),
            pltpu.SemaphoreType.DMA((n,)),
            pltpu.SemaphoreType.DMA((n,)),
            pltpu.SemaphoreType.DMA((n,)),
            pltpu.SemaphoreType.DMA((2,)),
            pltpu.SemaphoreType.DMA((2,)),
            pltpu.SemaphoreType.DMA,
        ],
        compiler_params=pltpu.CompilerParams(collective_id=0, has_side_effects=True),
        name="gather",
    )(w, f)


def compute_kernel(
    n, rows, chunks, lanes, channels, rooms,
    main_ref, prev_ref, next_ref, top_ref, bottom_ref, shift_ref, w_ref, mix_ref, mixt_ref, table_ref, tablet_ref, cot_ref,
    out_ref, parts_ref, gtable_ref,
    cols_ref, wide_ref, grad_ref, gmix_ref,
):
    image = pl.program_id(0)
    chunk = pl.program_id(1)
    first = jnp.logical_and(image == 0, chunk == 0)
    last = jnp.logical_and(image == pl.num_programs(0) - 1, chunk == chunks - 1)
    span = main_ref.shape[2]

    @pl.when(first)
    def _():
        wide_ref[...] = jnp.zeros_like(wide_ref)
        grad_ref[...] = jnp.zeros_like(grad_ref)
        gmix_ref[...] = jnp.zeros_like(gmix_ref)
        for tap in range(9):
            base = tap * lanes
            control = w_ref[10 + tap]
            wide_ref[base : base + channels, 0:channels] = w_ref[tap]
            wide_ref[base : base + channels, lanes : lanes + channels] = control
            wide_ref[base + channels : base + channels + rooms, lanes : lanes + channels] = jnp.dot(
                table_ref[...], control, preferred_element_type=jnp.float32
            ).astype(jnp.bfloat16)

    above = jnp.where(chunk == 0, top_ref[0], prev_ref[0, 0])
    below = jnp.where(chunk == chunks - 1, bottom_ref[0], next_ref[0, 0])
    spot = lax.broadcasted_iota(jnp.int32, (span, lanes), 0)
    for row in range(rows + 2):
        if row == 0:
            here = above
        elif row == rows + 1:
            here = below
        else:
            here = main_ref[0, row - 1]
        wide = here.astype(jnp.float32)
        shifted = (
            jnp.where(spot == 0, 0.0, pltpu.roll(wide, 1, 0)).astype(jnp.bfloat16),
            here,
            jnp.where(spot == span - 1, 0.0, pltpu.roll(wide, span - 1, 0)).astype(jnp.bfloat16),
        )
        for tap_row in range(3):
            spot_row = row - tap_row
            if 0 <= spot_row < rows:
                for tap_col in range(3):
                    base = (tap_row * 3 + tap_col) * lanes
                    cols_ref[spot_row * span : (spot_row + 1) * span, base : base + lanes] = shifted[tap_col]

    cells = rows * span
    cot = cot_ref[0].reshape(cells, channels)
    pre = jnp.dot(cols_ref[...], wide_ref[...], preferred_element_type=jnp.float32)
    shift = shift_ref[0]
    trunk = pre[:, :lanes] + shift
    control = pre[:, lanes:] + shift
    gate = 0.5 + 0.5 * jnp.tanh(0.5 * control)
    gated = (control * gate).astype(jnp.bfloat16)
    back = jnp.dot(cot, mixt_ref[...], preferred_element_type=jnp.float32)
    back_pre = (back * gate * (1.0 + control * (1.0 - gate))).astype(jnp.bfloat16)
    mixed = jnp.dot(gated, mix_ref[...], preferred_element_type=jnp.float32)
    trunk = trunk * (0.5 + 0.5 * jnp.tanh(0.5 * trunk))
    out = trunk[:, :channels] + mixed
    out_ref[0] = out.astype(jnp.bfloat16).reshape(rows, span, channels)
    back_t = back_pre.T[:channels]
    gated_t = gated.T[:channels]
    gmix_ref[...] += jnp.dot(gated_t, cot, preferred_element_type=jnp.float32)
    for tap_row in range(3):
        base = tap_row * 3 * lanes
        grad_ref[:, base : base + 3 * lanes] += jnp.dot(
            back_t, cols_ref[:, base : base + 3 * lanes], preferred_element_type=jnp.float32
        )

    @pl.when(last)
    def _():
        share = channels // n

        def put(tap, block):
            for owner in range(n):
                parts_ref[owner, tap] = block[owner * share : (owner + 1) * share].astype(parts_ref.dtype)

        total = jnp.zeros((2 * rooms, channels), jnp.float32)
        for tap in range(9):
            base = tap * lanes
            block = grad_ref[:, base : base + lanes].T
            room = block[channels : channels + rooms]
            high = room.astype(jnp.bfloat16)
            low = (room - high.astype(jnp.float32)).astype(jnp.bfloat16)
            pair = jnp.concatenate([high, low], axis=0)
            put(tap, block[:channels] + jnp.dot(tablet_ref[...], pair, preferred_element_type=jnp.float32))
            total = total + lax.dot_general(
                pair, w_ref[10 + tap], (((1,), (1,)), ((), ())), preferred_element_type=jnp.float32
            )
        put(9, gmix_ref[...])
        gtable_ref[...] = total[:rooms] + total[rooms:]


def compute(n, frame, top, bottom, shift, weights, mix, mixt, table, cotangent, rows):
    images, height, span, lanes = frame.shape
    channels = cotangent.shape[3]
    rooms = table.shape[0]
    chunks = height // rows
    tablet = jnp.concatenate([table.T, table.T], axis=1)

    def whole(array):
        return pl.BlockSpec(array.shape, lambda b, h: (0,) * array.ndim, pipeline_mode=pl.Buffered(1))

    return pl.pallas_call(
        functools.partial(compute_kernel, n, rows, chunks, lanes, channels, rooms),
        grid=(images, chunks),
        out_shape=(
            jax.ShapeDtypeStruct((images, height, span, channels), jnp.bfloat16),
            jax.ShapeDtypeStruct((n, 10, channels // n, channels), jnp.bfloat16),
            jax.ShapeDtypeStruct((rooms, channels), jnp.float32),
        ),
        in_specs=[
            pl.BlockSpec((1, rows, span, lanes), lambda b, h: (b, h, 0, 0)),
            pl.BlockSpec((1, 1, span, lanes), lambda b, h: (b, jnp.maximum(h * rows - 1, 0), 0, 0)),
            pl.BlockSpec((1, 1, span, lanes), lambda b, h: (b, jnp.minimum((h + 1) * rows, height - 1), 0, 0)),
            pl.BlockSpec((1, span, lanes), lambda b, h: (b, 0, 0)),
            pl.BlockSpec((1, span, lanes), lambda b, h: (b, 0, 0)),
            pl.BlockSpec((1, 1, lanes), lambda b, h: (b, 0, 0)),
            whole(weights),
            whole(mix),
            whole(mixt),
            whole(table),
            whole(tablet),
            pl.BlockSpec((1, rows, span, channels), lambda b, h: (b, h, 0, 0)),
        ],
        out_specs=(
            pl.BlockSpec((1, rows, span, channels), lambda b, h: (b, h, 0, 0)),
            pl.BlockSpec((n, 10, channels // n, channels), lambda b, h: (0, 0, 0, 0), pipeline_mode=pl.Buffered(1)),
            pl.BlockSpec((rooms, channels), lambda b, h: (0, 0)),
        ),
        scratch_shapes=[
            pltpu.VMEM((rows * span, 9 * lanes), jnp.bfloat16),
            pltpu.VMEM((9 * lanes, 2 * lanes), jnp.bfloat16),
            pltpu.VMEM((channels, 9 * lanes), jnp.float32),
            pltpu.VMEM((channels, channels), jnp.float32),
        ],
        compiler_params=pltpu.CompilerParams(vmem_limit_bytes=56 * MIB),
        cost_estimate=pl.CostEstimate(flops=60 * 10**9, bytes_accessed=20 * 10**6, transcendentals=4 * 10**6),
        name="convolve",
    )(frame, frame, frame, top, bottom, shift, weights, mix, mixt, table, tablet, cotangent)


def reduce_kernel(n, parts_ref, out_ref, other, inbox, outbox, final, pair_sems, send_sems, recv_sems, last_sems):
    me = lax.axis_index("mp")
    core = lax.axis_index("dp")
    pos = ring_position(me, n)
    right = {"mp": ring_index((pos + 1) % n, n)}
    left = {"mp": ring_index((pos + n - 1) % n, n)}
    sibling = {"dp": 1 - core}
    signal_all((right, left, sibling))
    half = parts_ref.shape[1] // 2
    mine = pl.ds(core * half, half)
    theirs = pl.ds((1 - core) * half, half)

    def remote(src, dst, send, recv, target):
        return pltpu.make_async_remote_copy(
            src_ref=src, dst_ref=dst, send_sem=send, recv_sem=recv, device_id=target, device_id_type=MESH
        )

    right_steps = n // 2
    left_steps = n - 1 - right_steps
    order = []
    for step in range(right_steps):
        order.append((0, step))
        if step < left_steps:
            order.append((1, step))

    def goal(side, step):
        if side == 0:
            return ring_index((pos + right_steps - step) % n, n)
        return ring_index((pos + n - left_steps + step) % n, n)

    pairs = {}
    for spot, key in enumerate(order + [None]):
        owner = me if key is None else goal(*key)
        copy = remote(
            parts_ref.at[owner, theirs], other.at[owner], pair_sems.at[0, spot], pair_sems.at[1, spot], sibling
        )
        copy.start()
        pairs[key] = copy

    ring = {}
    for side, step in order:
        owner = goal(side, step)
        pairs[side, step].wait_recv()
        total = parts_ref[owner, mine].astype(jnp.float32) + other[owner].astype(jnp.float32)
        slot = side * right_steps + step
        if step:
            ring[side, step - 1].wait_recv()
            total = total + inbox[slot - 1].astype(jnp.float32)
        outbox[slot] = total.astype(outbox.dtype)
        copy = remote(
            outbox.at[slot], inbox.at[slot], send_sems.at[slot], recv_sems.at[slot], (right, left)[side]
        )
        copy.start()
        ring[side, step] = copy
    pairs[None].wait_recv()
    total = parts_ref[me, mine].astype(jnp.float32) + other[me].astype(jnp.float32)
    for side, steps in ((1, left_steps), (0, right_steps)):
        if steps:
            ring[side, steps - 1].wait_recv()
            total = total + inbox[side * right_steps + steps - 1].astype(jnp.float32)
    final[...] = total
    swap = remote(final, out_ref.at[mine], last_sems.at[0], last_sems.at[1], sibling)
    swap.start()
    keep = pltpu.make_async_copy(final, out_ref.at[mine], last_sems.at[2])
    keep.start()
    for copy in pairs.values():
        copy.wait_send()
    for copy in ring.values():
        copy.wait_send()
    keep.wait()
    swap.wait()


def reduce(n, parts):
    _, count, share, channels = parts.shape
    half = count // 2
    return pl.pallas_call(
        functools.partial(reduce_kernel, n),
        out_shape=jax.ShapeDtypeStruct((count, share, channels), jnp.float32),
        in_specs=[pl.BlockSpec(memory_space=pltpu.VMEM)],
        out_specs=pl.BlockSpec(memory_space=pl.ANY),
        scratch_shapes=[
            pltpu.VMEM((n, half, share, channels), jnp.bfloat16),
            pltpu.VMEM((n, half, share, channels), jnp.bfloat16),
            pltpu.VMEM((n, half, share, channels), jnp.bfloat16),
            pltpu.VMEM((half, share, channels), jnp.float32),
            pltpu.SemaphoreType.DMA((2, n)),
            pltpu.SemaphoreType.DMA((n,)),
            pltpu.SemaphoreType.DMA((n,)),
            pltpu.SemaphoreType.DMA((3,)),
        ],
        compiler_params=pltpu.CompilerParams(
            collective_id=1, has_side_effects=True, vmem_limit_bytes=40 * MIB
        ),
        cost_estimate=pl.CostEstimate(flops=10**9, bytes_accessed=50 * 10**6, transcendentals=0),
        name="scatter",
    )(parts)


def sinusoid(timesteps, embed_width):
    half_width = embed_width // 2
    indices = jnp.arange(half_width, dtype=jnp.float32)
    frequency = jnp.exp(-math.log(10000.0) * indices / half_width)
    angles = timesteps.astype(jnp.float32)[:, None] * frequency[None, :]
    return jnp.concatenate([jnp.cos(angles), jnp.sin(angles)], axis=1)


def per_device(
    n,
    latents,
    room_labels,
    timesteps,
    label_table,
    time_weight,
    trunk_weight,
    control_weight,
    mix_weight,
    cotangent,
):
    images, height, span, channels = latents.shape
    rooms = label_table.shape[0]
    share = trunk_weight.shape[0]
    lanes = -(-(channels + rooms) // LANES) * LANES
    onehot = (room_labels[..., None] == jnp.arange(lanes - channels, dtype=jnp.int32)).astype(jnp.bfloat16)
    frame = jnp.concatenate([latents, onehot], axis=-1)

    def by_tap(weight):
        return weight.reshape(share, 9, channels).transpose(1, 0, 2)

    packed = jnp.concatenate(
        [by_tap(trunk_weight), mix_weight[None], by_tap(control_weight), mix_weight[None]], axis=0
    )
    gathered, halo = gather(n, packed, frame)
    weights = gathered.transpose(1, 0, 2, 3).reshape(20, n * share, channels)
    me = lax.axis_index("mp")
    top = jnp.where(me == 0, 0, halo[0])
    bottom = jnp.where(me == n - 1, 0, halo[1])
    time_features = jax.nn.silu(sinusoid(timesteps, time_weight.shape[0])).astype(jnp.bfloat16)
    time_shift = jnp.dot(time_features, time_weight, preferred_element_type=jnp.float32)
    time_shift = jnp.pad(time_shift, ((0, 0), (0, lanes - channels)))[:, None, :]
    mix = jnp.pad(weights[9], ((0, lanes - channels), (0, 0)))
    output, parts, table_local = compute(
        n, frame, top, bottom, time_shift, weights, mix, mix.T, label_table, cotangent, min(8, height)
    )
    grad_table = lax.psum(table_local, ("mp", "dp"))
    rows = reduce(n, parts)
    grad_control = rows[:9].transpose(1, 0, 2).reshape(share, 3, 3, channels)
    return (output, grad_control, rows[9], grad_table)


def solution(mesh):
    in_specs = (
        P(("groups", "dp"), "mp", None, None),
        P(("groups", "dp"), "mp", None),
        P(("groups", "dp")),
        P(),
        P(),
        P("mp", None, None, None),
        P("mp", None, None, None),
        P("mp", None),
        P(("groups", "dp"), "mp", None, None),
    )
    out_specs = (
        P(("groups", "dp"), "mp", None, None),
        P(("groups", "mp"), None, None, None),
        P(("groups", "mp"), None),
        P("groups", None),
    )
    return jax.shard_map(
        functools.partial(per_device, mesh.shape["mp"]),
        mesh=mesh,
        in_specs=in_specs,
        out_specs=out_specs,
        check_vma=False,
    )
```

time: 461 us -> 259 us (0.56)
  matrix products: 278 us -> 0.28 us
  Pallas kernels: 0 us -> 151 us
  blocking collectives: 107 us -> 61 us
  between operations: 14.4 us -> 0.72 us
  other arithmetic: 27.1 us -> 13.7 us
  local copies, waits for them, and re-layouts: 20.5 us -> 31 us
  starting transfers between devices: 9.47 us -> 0 us
    dot_general x41 -> x0, matrix products: 277 us -> none  [the longest x18 154 us: forward_taps(): jnp.einsum('bhwc,cd->bhwd', frame[:, tap_row:tap_row + row_count, tap_col...]
    pallas_call x0 -> x3, Pallas kernels: none -> 151 us  [the longest x1 83.7 us: compute(): pl.pallas_call(functools.partial(compute_kernel, n, rows, chunks, lanes,...]
    all_gather x1 -> x0, blocking collectives: 49.6 us -> none  [per_device(): lax.all_gather(mix_weight, 'mp', axis=0, tiled=True)]
    concatenate x3, other arithmetic: 26.8 us -> 8.58 us  [the longest x1 5.75 us: per_device(): frame = jnp.concatenate([latents, onehot], axis=-1)]
    unnamed x45 -> x10, local copies, waits for them, and re-layouts: 4.92 us -> 20 us
    ppermute x4 -> x0, starting transfers between devices: 9.31 us -> none  [the longest x2 6.19 us: with_halo(): lax.ppermute(tail, axis, [(i, (i + 1) % count) for i in range(ends)])]
    transpose x0 -> x2, local copies, waits for them, and re-layouts: none -> 6.27 us  [the longest x1 5.56 us: per_device(): weights = gathered.transpose(1, 0, 2, 3).reshape(20, n * share, channels)]
    squeeze x1 -> x2, local copies, waits for them, and re-layouts: 6.97 us -> 0.82 us  [the longest x1 0.63 us: per_device(): return (output, grad_control, rows[9], grad_table)]
  transfers between devices with their start and end apart: 8 -> 0, of which waited for: 0 -> 0; matrix products, arithmetic and copies ran while one was open for 69% -> 0% of each run, Pallas kernels for 0% -> 0%
where the time goes in v1:
time: 259 us; the launch traced here: 258 us
  Pallas kernels  151 us (58%)
  blocking collectives  61 us (24%)
  local copies, waits for them, and re-layouts  31 us (12%)
  other arithmetic  13.7 us (5%)
    pallas_call x1, Pallas kernels, compute(): pl.pallas_call(functools.partial(compute_kernel, n, rows, chunks, lanes,...  83.7 us
    psum x1, blocking collectives, per_device(): grad_table = lax.psum(table_local, ('mp', 'dp'))  61 us
    pallas_call x1, Pallas kernels, gather(): pl.pallas_call(functools.partial(gather_kernel, n), out_shape=(jax.ShapeD...  46.1 us
    pallas_call x1, Pallas kernels, reduce(): pl.pallas_call(functools.partial(reduce_kernel, n), out_shape=jax.ShapeDt...  21.6 us
    unnamed x10, local copies, waits for them, and re-layouts  20 us
    concatenate x1, other arithmetic, per_device(): frame = jnp.concatenate([latents, onehot], axis=-1)  5.75 us
    transpose x1, local copies, waits for them, and re-layouts, per_device(): weights = gathered.transpose(1, 0, 2, 3).reshape(20, n * share, channels)  5.56 us

profile of v1, /device:TPU:0, one launch (start us, length us, event | category | flops | bytes accessed | tf_op | source)
XLA Modules:
  0.0 258.2 jit_solution(9062180594775404816)
XLA Ops:
  0.7 0.7 convert_element_type.17
  1.6 0.2 copy-done
  1.8 0.3 fusion.2
  2.1 0.6 broadcast_in_dim.18.shift_ref
  2.7 0.8 pad_maximum_fusion.2
  3.5 0.7 copy.31.tablet_ref
  4.3 2.0 pad_maximum_fusion.1.w_ref
  6.3 2.3 fusion
  8.6 6.5 %copy.27 = bf16[3,16,128,320]{3,2,1,0:T(8,128)(2,1)} copy(bf16[3,16,128,320]{2,3,1,0:T(8,128)(2,1)} %param.9) | data formatting | bytes 7864320 | tf_op args[0]
  15.1 5.8 %pad_maximum_fusion.f_ref.main_ref.prev_ref.next_ref = bf16[3,16,128,384]{3,2,1,0:T(8,128)(2,1)} fusion(bf16[3,16,128,64]{3,2,1,0:T(8,128)(2,1)S(1)} %fusion, bf16[3,16,128,320]{3,2,1,0:T(8,128)(2,1)} %copy.27), kind=kLoop, calls=%fused_computation | loop fusion | flops 9437184 | bytes 9437184 | tf_op jit(solution)/shard_map/concatenate | solution.py:397
  20.9 6.5 %copy.32.cot_ref = bf16[3,16,128,320]{3,2,1,0:T(8,128)(2,1)} copy(bf16[3,16,128,320]{2,3,1,0:T(8,128)(2,1)} %param.17) | data formatting | bytes 7864320 | tf_op args[8]
  27.3 46.1 %gather.1 = (bf16[8,20,40,320]{3,2,1,0:T(8,128)(2,1)}, bf16[2,3,128,384]{3,2,1,0:T(8,128)(2,1)}) custom-call(bf16[20,40,320]{2,1,0:T(8,128)(2,1)} %pad_maximum_fusion.1.w_ref, bf16[3,16,128,384]{3,2,1,0:T(8,128)(2,1)} %pad_maximum_fusion.f_ref.main_ref.prev_ref.next_ref), custom_call_target="tpu_custom_call" | custom-call | tf_op jit(solution)/shard_map/gather/pallas_call | solution.py:106
  73.5 1.9 select_bitcast_fusion
  75.4 1.0 slice.21
  76.4 5.6 %copy.28 = bf16[20,8,40,320]{3,2,1,0:T(8,128)(2,1)} copy(bf16[20,8,40,320]{3,2,0,1:T(8,128)(2,1)} %bitcast.24) | data formatting | bytes 8192000 | tf_op jit(solution)/shard_map/transpose | solution.py:406
  82.1 0.7 pad_bitcast_fusion.mixt_ref
  82.9 0.2 copy.34
  83.1 0.8 pad.9.clone.mix_ref
  83.8 83.7 %convolve.1 = (bf16[3,16,128,320]{3,2,1,0:T(8,128)(2,1)}, bf16[8,10,40,320]{3,2,1,0:T(8,128)(2,1)}, f32[16,320]{1,0:T(8,128)}) custom-call(bf16[3,16,128,384]{3,2,1,0:T(8,128)(2,1)} %pad_maximum_fusion.f_ref.main_ref.prev_ref.next_ref, bf16[3,16,128,384]{3,2,1,0:T(8,128)(2,1)} %pad_maximum_fusion.f_ref.main_ref.prev_ref.next_ref, ...), custom_call_target="tpu_custom_call" | custom-call | flops 60000002048 | bytes 20000000 | tf_op jit(solution)/shard_map/convolve/pallas_call | solution.py:234
  167.5 6.6 %copy.33 = bf16[3,16,128,320]{2,3,1,0:T(8,128)(2,1)} copy(bf16[3,16,128,320]{3,2,1,0:T(8,128)(2,1)} %get-tuple-element.22) | data formatting | bytes 7864320
  174.1 61.0 %psum.7 = f32[16,320]{1,0:T(8,128)} all-reduce(f32[16,320]{1,0:T(8,128)S(1)} %copy-done.2), channel_id=1, replica_groups=mesh['groups'=2,'mp'=8,'dp'=2] {'mp','dp'}, use_global_device_ids=true, to_apply=%region_0.1 | all-reduce | flops 5120 | bytes 40960 | tf_op jit(solution)/shard_map/psum | solution.py:417
  235.1 21.6 %scatter.1 = f32[10,40,320]{2,1,0:T(8,128)S(1)} custom-call(bf16[8,10,40,320]{3,2,1,0:T(8,128)(2,1)S(1)} %copy-done.1), custom_call_target="tpu_custom_call" | custom-call | flops 1000000000 | bytes 50000000 | tf_op jit(solution)/shard_map/scatter/pallas_call | solution.py:349
  256.8 0.6 slice_bitcast_fusion
  257.4 0.8 slice.19
  (9 shorter events, 0.4 us)
Async XLA Ops:
  0.6 1.2 copy-start
  167.5 6.6 %copy-start.2 = (f32[16,320]{1,0:T(8,128)S(1)}, f32[16,320]{1,0:T(8,128)}, u32[]{:S(2)}) copy-start(f32[16,320]{1,0:T(8,128)} %get-tuple-element.13) | copy-start | bytes 61444
  167.5 67.6 %copy-start.1 = (bf16[8,10,40,320]{3,2,1,0:T(8,128)(2,1)S(1)}, bf16[8,10,40,320]{3,2,1,0:T(8,128)(2,1)}, u32[]{:S(2)}) copy-start(bf16[8,10,40,320]{3,2,1,0:T(8,128)(2,1)} %get-tuple-element.12.parts_ref) | copy-start | bytes 6144004

commit v2 on v1

v2 whole, which is shorter than its diff:
```python
import functools
import math

import jax
import jax.numpy as jnp
from jax import lax
from jax.experimental import pallas as pl
from jax.experimental.pallas import tpu as pltpu
from jax.sharding import PartitionSpec as P

MESH = pl.DeviceIdType.MESH
LANES = 128
MIB = 1024 * 1024


def ring_position(index, count):
    if count != 8:
        return index
    short, long = index % 2, index // 2
    return (1 - short) * long + short * (count - 1 - long)


def ring_index(position, count):
    if count != 8:
        return position
    short = position // (count // 2)
    long = (1 - short) * position + short * (count - 1 - position)
    return 2 * long + short


def signal_all(targets):
    barrier = pltpu.get_barrier_semaphore()
    for target in targets:
        pl.semaphore_signal(barrier, inc=1, device_id=target, device_id_type=MESH)
    pl.semaphore_wait(barrier, len(targets))


def gather_kernel(
    n, pieces, w_ref, f_ref, e_ref, g_ref, halo_ref, edge_ref,
    ring_send, ring_recv, sib_send, sib_recv, halo_send, halo_recv, own_sem,
):
    me = lax.axis_index("mp")
    core = lax.axis_index("dp")
    pos = ring_position(me, n)
    right = {"mp": ring_index((pos + 1) % n, n)}
    left = {"mp": ring_index((pos + n - 1) % n, n)}
    up = {"mp": (me + n - 1) % n}
    down = {"mp": (me + 1) % n}
    sibling = {"dp": 1 - core}
    signal_all((right, left, up, down, sibling))
    half = w_ref.shape[0] // 2
    size = half // pieces
    rows = f_ref.shape[1]

    def remote(src, dst, send, recv, target):
        return pltpu.make_async_remote_copy(
            src_ref=src, dst_ref=dst, send_sem=send, recv_sem=recv, device_id=target, device_id_type=MESH
        )

    right_steps = n // 2
    left_steps = n - 1 - right_steps
    pending = []
    ring = {}

    def send(side, step, piece):
        shift = n - step if side == 0 else step
        origin = ring_index((pos + shift) % n, n)
        part = pl.ds(core * half + piece * size, size)
        src = w_ref.at[part] if step == 0 else g_ref.at[origin, part]
        slot = side * right_steps + step
        copy = remote(
            src, g_ref.at[origin, part], ring_send.at[slot, piece], ring_recv.at[slot, piece], (right, left)[side]
        )
        copy.start()
        ring[side, step, piece] = copy

    for piece in range(pieces):
        send(0, 0, piece)
        if left_steps:
            send(1, 0, piece)
    edges = [
        remote(f_ref.at[:, rows - 1], halo_ref.at[0], halo_send.at[0], halo_recv.at[0], down),
        remote(f_ref.at[:, 0], halo_ref.at[1], halo_send.at[1], halo_recv.at[1], up),
        remote(e_ref.at[0], edge_ref.at[0], halo_send.at[2], halo_recv.at[2], down),
        remote(e_ref.at[1], edge_ref.at[1], halo_send.at[3], halo_recv.at[3], up),
    ]
    for copy in edges:
        copy.start()
    own = pltpu.make_async_copy(w_ref, g_ref.at[me], own_sem)
    own.start()
    for step in range(right_steps):
        for piece in range(pieces):
            for side, steps in ((0, right_steps), (1, left_steps)):
                if step >= steps:
                    continue
                ring[side, step, piece].wait_recv()
                if step + 1 < steps:
                    send(side, step + 1, piece)
                shift = n - step - 1 if side == 0 else step + 1
                origin = ring_index((pos + shift) % n, n)
                slot = side * right_steps + step
                part = pl.ds(core * half + piece * size, size)
                copy = remote(
                    g_ref.at[origin, part], g_ref.at[origin, part],
                    sib_send.at[slot, piece], sib_recv.at[slot, piece], sibling,
                )
                copy.start()
                pending.append(copy)
    for copy in ring.values():
        copy.wait_send()
    for copy in pending + edges:
        copy.wait()
    own.wait()


def gather(n, w, f, e):
    images, _, depth, span = f.shape
    pieces = 2 if w.shape[0] % 4 == 0 else 1
    return pl.pallas_call(
        functools.partial(gather_kernel, n, pieces),
        out_shape=(
            jax.ShapeDtypeStruct((n,) + w.shape, w.dtype),
            jax.ShapeDtypeStruct((2, images, depth, span), f.dtype),
            jax.ShapeDtypeStruct(e.shape, e.dtype),
        ),
        in_specs=[pl.BlockSpec(memory_space=pl.ANY)] * 3,
        out_specs=(pl.BlockSpec(memory_space=pl.ANY),) * 3,
        scratch_shapes=[
            pltpu.SemaphoreType.DMA((n, pieces)),
            pltpu.SemaphoreType.DMA((n, pieces)),
            pltpu.SemaphoreType.DMA((n, pieces)),
            pltpu.SemaphoreType.DMA((n, pieces)),
            pltpu.SemaphoreType.DMA((4,)),
            pltpu.SemaphoreType.DMA((4,)),
            pltpu.SemaphoreType.DMA,
        ],
        compiler_params=pltpu.CompilerParams(collective_id=0, has_side_effects=True),
        name="gather",
    )(w, f, e)


def compute_kernel(
    n, rows, chunks, lanes, channels, rooms,
    me_ref, main_ref, prev_ref, next_ref, halo_ref, label_ref, edge_ref, shift_ref, w_ref, table_ref, tablet_ref, cot_in_ref,
    out_ref, parts_ref, gtable_ref,
    cols_ref, wide_ref, mix_ref, mixt_ref, cot_ref, grad_ref, gmix_ref,
):
    image = pl.program_id(0)
    chunk = pl.program_id(1)
    first = jnp.logical_and(image == 0, chunk == 0)
    last = jnp.logical_and(image == pl.num_programs(0) - 1, chunk == chunks - 1)
    span = main_ref.shape[3]
    height = rows * chunks

    def weight(tap):
        return w_ref[:, tap].astype(jnp.float32).reshape(channels, channels)

    @pl.when(first)
    def _():
        wide_ref[...] = jnp.zeros_like(wide_ref)
        grad_ref[...] = jnp.zeros_like(grad_ref)
        gmix_ref[...] = jnp.zeros_like(gmix_ref)
        mix_ref[...] = jnp.zeros_like(mix_ref)
        mixt_ref[...] = jnp.zeros_like(mixt_ref)
        mix = weight(9)
        mix_ref[0:channels] = mix.astype(jnp.bfloat16)
        mixt_ref[:, 0:channels] = mix.T.astype(jnp.bfloat16)
        for tap in range(9):
            base = tap * lanes
            control = weight(10 + tap).astype(jnp.bfloat16)
            wide_ref[base : base + channels, 0:channels] = weight(tap).astype(jnp.bfloat16)
            wide_ref[base : base + channels, lanes : lanes + channels] = control
            wide_ref[base + channels : base + channels + rooms, lanes : lanes + channels] = jnp.dot(
                table_ref[...], control, preferred_element_type=jnp.float32
            ).astype(jnp.bfloat16)

    spot = lax.broadcasted_iota(jnp.int32, (span, lanes), 0)
    slot = lax.broadcasted_iota(jnp.int32, (lanes - channels, span), 0)
    for row in range(rows + 2):
        if 0 < row <= rows:
            here = main_ref[0, row - 1]
            label = label_ref[0, pl.ds(chunk * rows + row - 1, 1)]
        else:
            side = 0 if row == 0 else 1
            outside = chunk == (0, chunks - 1)[side]
            dead = jnp.logical_and(outside, me_ref[0] == (0, n - 1)[side])
            beyond = jnp.clip(chunk * rows + row - 1, 0, height - 1)
            here = jnp.where(outside, halo_ref[side, 0], (prev_ref, next_ref)[side][0, 0])
            here = jnp.where(dead, jnp.zeros_like(here), here)
            label = jnp.where(outside, edge_ref[side, 0, 0:1], label_ref[0, pl.ds(beyond, 1)])
            label = jnp.where(dead, -1, label)
        onehot = jnp.where(slot == label, 1.0, 0.0).astype(jnp.bfloat16)
        here = jnp.concatenate([here, onehot], axis=0).T
        wide = here.astype(jnp.float32)
        shifted = (
            jnp.where(spot == 0, 0.0, pltpu.roll(wide, 1, 0)).astype(jnp.bfloat16),
            here,
            jnp.where(spot == span - 1, 0.0, pltpu.roll(wide, span - 1, 0)).astype(jnp.bfloat16),
        )
        for tap_row in range(3):
            spot_row = row - tap_row
            if 0 <= spot_row < rows:
                for tap_col in range(3):
                    base = (tap_row * 3 + tap_col) * lanes
                    cols_ref[spot_row * span : (spot_row + 1) * span, base : base + lanes] = shifted[tap_col]
    for row in range(rows):
        cot_ref[row * span : (row + 1) * span] = cot_in_ref[0, row].T

    cot = cot_ref[...]
    pre = jnp.dot(cols_ref[...], wide_ref[...], preferred_element_type=jnp.float32)
    shift = shift_ref[0]
    trunk = pre[:, :lanes] + shift
    control = pre[:, lanes:] + shift
    gate = 0.5 + 0.5 * jnp.tanh(0.5 * control)
    gated = (control * gate).astype(jnp.bfloat16)
    back = jnp.dot(cot, mixt_ref[...], preferred_element_type=jnp.float32)
    back_pre = (back * gate * (1.0 + control * (1.0 - gate))).astype(jnp.bfloat16)
    mixed = jnp.dot(gated, mix_ref[...], preferred_element_type=jnp.float32)
    trunk = trunk * (0.5 + 0.5 * jnp.tanh(0.5 * trunk))
    out = (trunk[:, :channels] + mixed).astype(jnp.bfloat16)
    for row in range(rows):
        out_ref[0, row] = out[row * span : (row + 1) * span].T
    back_t = back_pre.T[:channels]
    gated_t = gated.T[:channels]
    gmix_ref[...] += jnp.dot(gated_t, cot, preferred_element_type=jnp.float32)
    for tap_row in range(3):
        base = tap_row * 3 * lanes
        grad_ref[:, base : base + 3 * lanes] += jnp.dot(
            back_t, cols_ref[:, base : base + 3 * lanes], preferred_element_type=jnp.float32
        )

    @pl.when(last)
    def _():
        share = channels // n

        def put(tap, block):
            for owner in range(n):
                parts_ref[owner, tap] = block[owner * share : (owner + 1) * share].astype(parts_ref.dtype)

        total = jnp.zeros((2 * rooms, channels), jnp.float32)
        for tap in range(9):
            base = tap * lanes
            block = grad_ref[:, base : base + lanes].T
            room = block[channels : channels + rooms]
            high = room.astype(jnp.bfloat16)
            low = (room - high.astype(jnp.float32)).astype(jnp.bfloat16)
            pair = jnp.concatenate([high, low], axis=0)
            put(tap, block[:channels] + jnp.dot(tablet_ref[...], pair, preferred_element_type=jnp.float32))
            total = total + lax.dot_general(
                pair, wide_ref[base : base + channels, lanes : lanes + channels], (((1,), (1,)), ((), ())),
                preferred_element_type=jnp.float32,
            )
        put(9, gmix_ref[...])
        gtable_ref[...] = total[:rooms] + total[rooms:]


def compute(n, me, latents, halo, labels, edge, shift, weights, table, cotangent, rows, lanes):
    images, height, channels, span = latents.shape
    rooms = table.shape[0]
    chunks = height // rows
    tablet = jnp.concatenate([table.T, table.T], axis=1)

    def whole(array):
        return pl.BlockSpec(array.shape, lambda b, h: (0,) * array.ndim, pipeline_mode=pl.Buffered(1))

    return pl.pallas_call(
        functools.partial(compute_kernel, n, rows, chunks, lanes, channels, rooms),
        grid=(images, chunks),
        out_shape=(
            jax.ShapeDtypeStruct((images, height, channels, span), jnp.bfloat16),
            jax.ShapeDtypeStruct((n, 10, channels // n, channels), jnp.bfloat16),
            jax.ShapeDtypeStruct((rooms, channels), jnp.float32),
        ),
        in_specs=[
            pl.BlockSpec(memory_space=pltpu.SMEM),
            pl.BlockSpec((1, rows, channels, span), lambda b, h: (b, h, 0, 0)),
            pl.BlockSpec((1, 1, channels, span), lambda b, h: (b, jnp.maximum(h * rows - 1, 0), 0, 0)),
            pl.BlockSpec((1, 1, channels, span), lambda b, h: (b, jnp.minimum((h + 1) * rows, height - 1), 0, 0)),
            pl.BlockSpec((2, 1, channels, span), lambda b, h: (0, b, 0, 0)),
            pl.BlockSpec((1, height, span), lambda b, h: (b, 0, 0)),
            pl.BlockSpec((2, 1, 8, span), lambda b, h: (0, b, 0, 0)),
            pl.BlockSpec((1, 1, lanes), lambda b, h: (b, 0, 0)),
            whole(weights),
            whole(table),
            whole(tablet),
            pl.BlockSpec((1, rows, channels, span), lambda b, h: (b, h, 0, 0)),
        ],
        out_specs=(
            pl.BlockSpec((1, rows, channels, span), lambda b, h: (b, h, 0, 0)),
            pl.BlockSpec((n, 10, channels // n, channels), lambda b, h: (0, 0, 0, 0), pipeline_mode=pl.Buffered(1)),
            pl.BlockSpec((rooms, channels), lambda b, h: (0, 0)),
        ),
        scratch_shapes=[
            pltpu.VMEM((rows * span, 9 * lanes), jnp.bfloat16),
            pltpu.VMEM((9 * lanes, 2 * lanes), jnp.bfloat16),
            pltpu.VMEM((lanes, channels), jnp.bfloat16),
            pltpu.VMEM((channels, lanes), jnp.bfloat16),
            pltpu.VMEM((rows * span, channels), jnp.bfloat16),
            pltpu.VMEM((channels, 9 * lanes), jnp.float32),
            pltpu.VMEM((channels, channels), jnp.float32),
        ],
        compiler_params=pltpu.CompilerParams(vmem_limit_bytes=56 * MIB),
        cost_estimate=pl.CostEstimate(flops=60 * 10**9, bytes_accessed=20 * 10**6, transcendentals=4 * 10**6),
        name="convolve",
    )(me, latents, latents, latents, halo, labels, edge, shift, weights, table, tablet, cotangent)


def reduce_kernel(
    n, parts_ref, table_ref, out_ref, sums_ref, other, inbox, outbox, final, table_other, table_both, table_in, table_sum,
    pair_sems, send_sems, recv_sems, last_sems, table_send, table_recv,
):
    me = lax.axis_index("mp")
    core = lax.axis_index("dp")
    pos = ring_position(me, n)
    right = {"mp": ring_index((pos + 1) % n, n)}
    left = {"mp": ring_index((pos + n - 1) % n, n)}
    sibling = {"dp": 1 - core}
    others = [{"mp": (me + step) % n} for step in range(1, n)]
    signal_all(others + [sibling])
    half = parts_ref.shape[1] // 2
    mine = pl.ds(core * half, half)
    theirs = pl.ds((1 - core) * half, half)

    def remote(src, dst, send, recv, target):
        return pltpu.make_async_remote_copy(
            src_ref=src, dst_ref=dst, send_sem=send, recv_sem=recv, device_id=target, device_id_type=MESH
        )

    right_steps = n // 2
    left_steps = n - 1 - right_steps
    order = []
    for step in range(right_steps):
        order.append((0, step))
        if step < left_steps:
            order.append((1, step))

    def goal(side, step):
        if side == 0:
            return ring_index((pos + right_steps - step) % n, n)
        return ring_index((pos + n - left_steps + step) % n, n)

    table_swap = remote(table_ref, table_other, table_send.at[0], table_recv.at[0], sibling)
    table_swap.start()
    pairs = {}
    for spot, key in enumerate(order + [None]):
        owner = me if key is None else goal(*key)
        copy = remote(
            parts_ref.at[owner, theirs], other.at[owner], pair_sems.at[0, spot], pair_sems.at[1, spot], sibling
        )
        copy.start()
        pairs[key] = copy

    table_swap.wait_recv()
    table_both[...] = table_ref[...] + table_other[...]
    table_half = table_ref.shape[0] // 2
    table_mine = pl.ds(pl.multiple_of(core * table_half, table_half), table_half)
    table_in[me] = table_both[table_mine]
    spread = []
    for spot, target in enumerate(others):
        copy = remote(
            table_both.at[table_mine], table_in.at[me], table_send.at[1 + spot], table_recv.at[1 + spot], target
        )
        copy.start()
        spread.append(copy)

    ring = {}
    for side, step in order:
        owner = goal(side, step)
        pairs[side, step].wait_recv()
        total = parts_ref[owner, mine].astype(jnp.float32) + other[owner].astype(jnp.float32)
        slot = side * right_steps + step
        if step:
            ring[side, step - 1].wait_recv()
            total = total + inbox[slot - 1].astype(jnp.float32)
        outbox[slot] = total.astype(outbox.dtype)
        copy = remote(
            outbox.at[slot], inbox.at[slot], send_sems.at[slot], recv_sems.at[slot], (right, left)[side]
        )
        copy.start()
        ring[side, step] = copy
    pairs[None].wait_recv()
    total = parts_ref[me, mine].astype(jnp.float32) + other[me].astype(jnp.float32)
    for side, steps in ((1, left_steps), (0, right_steps)):
        if steps:
            ring[side, steps - 1].wait_recv()
            total = total + inbox[side * right_steps + steps - 1].astype(jnp.float32)
    final[...] = total
    swap = remote(final, out_ref.at[mine], last_sems.at[0], last_sems.at[1], sibling)
    swap.start()
    keep = pltpu.make_async_copy(final, out_ref.at[mine], last_sems.at[2])
    keep.start()
    for spot in range(1, n):
        source = (me + n - spot) % n
        remote(
            table_both.at[table_mine], table_in.at[source], table_send.at[spot], table_recv.at[spot], others[0]
        ).wait_recv()
    table = table_in[0]
    for source in range(1, n):
        table = table + table_in[source]
    table_sum[...] = table
    sums_swap = remote(table_sum, sums_ref.at[table_mine], last_sems.at[3], last_sems.at[4], sibling)
    sums_swap.start()
    sums_keep = pltpu.make_async_copy(table_sum, sums_ref.at[table_mine], last_sems.at[5])
    sums_keep.start()
    table_swap.wait_send()
    for copy in spread:
        copy.wait_send()
    sums_keep.wait()
    sums_swap.wait()
    for copy in pairs.values():
        copy.wait_send()
    for copy in ring.values():
        copy.wait_send()
    keep.wait()
    swap.wait()


def reduce(n, parts, table):
    _, count, share, channels = parts.shape
    half = count // 2
    return pl.pallas_call(
        functools.partial(reduce_kernel, n),
        out_shape=(
            jax.ShapeDtypeStruct((count, share, channels), jnp.float32),
            jax.ShapeDtypeStruct(table.shape, jnp.float32),
        ),
        in_specs=[pl.BlockSpec(memory_space=pltpu.VMEM)] * 2,
        out_specs=(pl.BlockSpec(memory_space=pl.ANY),) * 2,
        scratch_shapes=[
            pltpu.VMEM((n, half, share, channels), jnp.bfloat16),
            pltpu.VMEM((n, half, share, channels), jnp.bfloat16),
            pltpu.VMEM((n, half, share, channels), jnp.bfloat16),
            pltpu.VMEM((half, share, channels), jnp.float32),
            pltpu.VMEM(table.shape, jnp.float32),
            pltpu.VMEM(table.shape, jnp.float32),
            pltpu.VMEM((n, table.shape[0] // 2, channels), jnp.float32),
            pltpu.VMEM((table.shape[0] // 2, channels), jnp.float32),
            pltpu.SemaphoreType.DMA((2, n)),
            pltpu.SemaphoreType.DMA((n,)),
            pltpu.SemaphoreType.DMA((n,)),
            pltpu.SemaphoreType.DMA((6,)),
            pltpu.SemaphoreType.DMA((n,)),
            pltpu.SemaphoreType.DMA((n,)),
        ],
        compiler_params=pltpu.CompilerParams(
            collective_id=1, has_side_effects=True, vmem_limit_bytes=40 * MIB
        ),
        cost_estimate=pl.CostEstimate(flops=10**9, bytes_accessed=50 * 10**6, transcendentals=0),
        name="scatter",
    )(parts, table)


def sinusoid(timesteps, embed_width):
    half_width = embed_width // 2
    indices = jnp.arange(half_width, dtype=jnp.float32)
    frequency = jnp.exp(-math.log(10000.0) * indices / half_width)
    angles = timesteps.astype(jnp.float32)[:, None] * frequency[None, :]
    return jnp.concatenate([jnp.cos(angles), jnp.sin(angles)], axis=1)


def per_device(
    n,
    latents,
    room_labels,
    timesteps,
    label_table,
    time_weight,
    trunk_weight,
    control_weight,
    mix_weight,
    cotangent,
):
    images, height, span, channels = latents.shape
    rooms = label_table.shape[0]
    share = trunk_weight.shape[0]
    lanes = -(-(channels + rooms) // LANES) * LANES
    columns = latents.transpose(0, 1, 3, 2)
    edge_out = jnp.stack([room_labels[:, height - 1], room_labels[:, 0]])
    edge_out = jnp.broadcast_to(edge_out[:, :, None, :], (2, images, 8, span))

    def by_tap(weight):
        return weight.reshape(share, 9, channels).transpose(1, 0, 2)

    packed = jnp.concatenate(
        [by_tap(trunk_weight), mix_weight[None], by_tap(control_weight), mix_weight[None]], axis=0
    )
    gathered, halo, edge = gather(n, packed, columns, edge_out)
    if share % 8:
        gathered = gathered.transpose(1, 0, 2, 3).reshape(1, 20, n * share, channels)
    me = lax.axis_index("mp")[None].astype(jnp.int32)
    time_features = jax.nn.silu(sinusoid(timesteps, time_weight.shape[0])).astype(jnp.bfloat16)
    time_shift = jnp.dot(time_features, time_weight, preferred_element_type=jnp.float32)
    time_shift = jnp.pad(time_shift, ((0, 0), (0, lanes - channels)))[:, None, :]
    output, parts, table_local = compute(
        n, me, columns, halo, room_labels, edge, time_shift, gathered, label_table,
        cotangent.transpose(0, 1, 3, 2), min(8, height), lanes,
    )
    rows, grad_table = reduce(n, parts, table_local)
    output = output.transpose(0, 1, 3, 2)
    grad_control = rows[:9].transpose(1, 0, 2).reshape(share, 3, 3, channels)
    return (output, grad_control, rows[9], grad_table)


def solution(mesh):
    in_specs = (
        P(("groups", "dp"), "mp", None, None),
        P(("groups", "dp"), "mp", None),
        P(("groups", "dp")),
        P(),
        P(),
        P("mp", None, None, None),
        P("mp", None, None, None),
        P("mp", None),
        P(("groups", "dp"), "mp", None, None),
    )
    out_specs = (
        P(("groups", "dp"), "mp", None, None),
        P(("groups", "mp"), None, None, None),
        P(("groups", "mp"), None),
        P("groups", None),
    )
    return jax.shard_map(
        functools.partial(per_device, mesh.shape["mp"]),
        mesh=mesh,
        in_specs=in_specs,
        out_specs=out_specs,
        check_vma=False,
    )
```

time: 259 us -> 168 us (0.65)
  blocking collectives: 61 us -> 0 us
  local copies, waits for them, and re-layouts: 31 us -> 7.25 us
  other arithmetic: 13.7 us -> 3.74 us
  Pallas kernels: 151 us -> 156 us
    psum x1 -> x0, blocking collectives: 61 us -> none  [per_device(): grad_table = lax.psum(table_local, ('mp', 'dp'))]
    unnamed x10 -> x7, local copies, waits for them, and re-layouts: 20 us -> 3.04 us
    transpose x2 -> x0, local copies, waits for them, and re-layouts: 6.27 us -> none  [the longest x1 5.56 us: per_device(): weights = gathered.transpose(1, 0, 2, 3).reshape(20, n * share, channels)]
    concatenate x1 -> x0, other arithmetic: 5.75 us -> none  [per_device(): frame = jnp.concatenate([latents, onehot], axis=-1)]
    pallas_call x2, Pallas kernels: 67.8 us -> 70.5 us  [the longest x1 44.7 us: gather(): pl.pallas_call(functools.partial(gather_kernel, n, pieces), out_shape=(ja...]
where the time goes in v2:
time: 168 us
  Pallas kernels  156 us (93%)
  local copies, waits for them, and re-layouts  7.25 us (4%)
  other arithmetic  3.74 us (2%)
    pallas_call x1, Pallas kernels, compute(): pl.pallas_call(functools.partial(compute_kernel, n, rows, chunks, lanes,...  85.4 us
    pallas_call x1, Pallas kernels, gather(): pl.pallas_call(functools.partial(gather_kernel, n, pieces), out_shape=(ja...  44.7 us
    pallas_call x1, Pallas kernels, reduce(): pl.pallas_call(functools.partial(reduce_kernel, n), out_shape=(jax.ShapeD...  25.9 us

profile of v2, /device:TPU:0, one launch (start us, length us, event | category | flops | bytes accessed | tf_op | source)
XLA Modules:
  0.0 167.9 jit_solution(6372140748303849705)
XLA Ops:
  0.6 0.0 copy-start
  0.7 0.7 convert_element_type.8
  1.4 0.7 slice_bitcast_fusion.2
  2.1 0.2 multiply_cosine_fusion
  2.3 0.0 copy-done
  2.3 0.3 fusion.1
  2.6 0.6 broadcast_in_dim.21.shift_ref
  3.3 0.6 broadcast_in_dim.20.e_ref
  3.9 0.8 pad_maximum_fusion.1
  4.7 0.7 copy.16.tablet_ref
  5.4 2.0 %pad_maximum_fusion.w_ref = bf16[20,40,320]{2,1,0:T(8,128)(2,1)} fusion(bf16[1,40,320]{2,1,0:T(8,128)(2,1)} %bitcast.29, bf16[9,40,320]{2,1,0:T(8,128)(2,1)} %bitcast.27, bf16[9,40,320]{2,1,0:T(8,128)(2,1)} %bitcast.28), kind=kLoop, calls=%fused_computation | loop fusion | flops 768000 | bytes 998400 | tf_op jit(solution)/shard_map/concatenate | solution.py:484
  7.4 44.7 %gather.1 = (bf16[8,20,40,320]{3,2,1,0:T(8,128)(2,1)}, bf16[2,3,320,128]{3,2,1,0:T(8,128)(2,1)}, s32[2,3,8,128]{3,2,1,0:T(8,128)}) custom-call(bf16[20,40,320]{2,1,0:T(8,128)(2,1)} %pad_maximum_fusion.w_ref, bf16[3,16,320,128]{3,2,1,0:T(8,128)(2,1)} %bitcast.22, s32[2,3,8,128]{3,2,1,0:T(8,128)} %broadcast_in_dim.20.e_ref), custom_call_target="tpu_custom_call" | custom-call | tf_op jit(solution)/shard_map/gather/pallas_call | solution.py:119
  52.1 85.4 %convolve.1 = (bf16[3,16,320,128]{3,2,1,0:T(8,128)(2,1)}, bf16[8,10,40,320]{3,2,1,0:T(8,128)(2,1)}, f32[16,320]{1,0:T(8,128)}) custom-call(s32[1]{0:T(128)} %bitcast.me_ref, bf16[3,16,320,128]{3,2,1,0:T(8,128)(2,1)} %bitcast.23, bf16[3,16,320,128]{3,2,1,0:T(8,128)(2,1)} %bitcast.24, bf16[3,16,320,128]{3,2,1,0:T(8,128)(2,1)} %bitcast.25, ...), custom_call_target="tpu_custom_call" | custom-call | flops 60000002048 | bytes 20000000 | tf_op jit(solution)/shard_map/convolve/pallas_call | solution.py:266
  137.5 0.0 copy-start.1
  137.5 1.7 %copy-done.1 = bf16[8,10,40,320]{3,2,1,0:T(8,128)(2,1)S(1)} copy-done((bf16[8,10,40,320]{3,2,1,0:T(8,128)(2,1)S(1)}, bf16[8,10,40,320]{3,2,1,0:T(8,128)(2,1)}, u32[]{:S(2)}) %copy-start.1) | copy-done | bytes 2048024
  139.2 0.0 copy-start.2
  139.2 0.7 copy-done.2
  140.0 25.9 %scatter.1 = (f32[10,40,320]{2,1,0:T(8,128)S(1)}, f32[16,320]{1,0:T(8,128)S(1)}) custom-call(bf16[8,10,40,320]{3,2,1,0:T(8,128)(2,1)S(1)} %copy-done.1, f32[16,320]{1,0:T(8,128)S(1)} %copy-done.2), custom_call_target="tpu_custom_call" | custom-call | flops 1000000000 | bytes 50000000 | tf_op jit(solution)/shard_map/scatter/pallas_call | solution.py:421
  165.8 0.6 slice_bitcast_fusion
  166.5 0.8 slice.14
  167.3 0.6 copy.18
  (4 shorter events, 0.0 us)
Async XLA Ops:
  0.6 1.7 copy-start
  137.5 1.7 %copy-start.1 = (bf16[8,10,40,320]{3,2,1,0:T(8,128)(2,1)S(1)}, bf16[8,10,40,320]{3,2,1,0:T(8,128)(2,1)}, u32[]{:S(2)}) copy-start(bf16[8,10,40,320]{3,2,1,0:T(8,128)(2,1)} %get-tuple-element.16.parts_ref) | copy-start | bytes 6144004
  139.2 0.7 copy-start.2

commit v3 on v2

--- a/solution.py
+++ b/solution.py
@@ -36,8 +36,8 @@
 
 
 def gather_kernel(
-    n, pieces, w_ref, f_ref, e_ref, g_ref, halo_ref, edge_ref,
-    ring_send, ring_recv, sib_send, sib_recv, halo_send, halo_recv, own_sem,
+    n, paired, w_ref, f_ref, e_ref, g_ref, halo_ref, edge_ref,
+    ring_send, ring_recv, sib_send, sib_recv, twin_send, twin_recv, halo_send, halo_recv, own_sem,
 ):
     me = lax.axis_index("mp")
     core = lax.axis_index("dp")
@@ -47,9 +47,20 @@
     up = {"mp": (me + n - 1) % n}
     down = {"mp": (me + 1) % n}
     sibling = {"dp": 1 - core}
-    signal_all((right, left, up, down, sibling))
+    targets = [right, left, up, down, sibling]
+    group = lax.axis_index("groups")
+    turn = group % 2
+    twin = {"groups": group + 1 - 2 * turn}
+    if paired:
+        targets.append(twin)
+    signal_all(targets)
     half = w_ref.shape[0] // 2
-    size = half // pieces
+    third = half // 3 if paired else 0
+    own_part = pl.ds(core * half + turn * (half - third), third)
+    twin_part = pl.ds(core * half + (1 - turn) * (half - third), third)
+    shared_part = pl.ds(core * half + third, half - 2 * third)
+    parts = (own_part, shared_part) if paired else (shared_part,)
+    pieces = len(parts)
     rows = f_ref.shape[1]
 
     def remote(src, dst, send, recv, target):
@@ -65,7 +76,7 @@
     def send(side, step, piece):
         shift = n - step if side == 0 else step
         origin = ring_index((pos + shift) % n, n)
-        part = pl.ds(core * half + piece * size, size)
+        part = parts[piece]
         src = w_ref.at[part] if step == 0 else g_ref.at[origin, part]
         slot = side * right_steps + step
         copy = remote(
@@ -73,6 +84,18 @@
         )
         copy.start()
         ring[side, step, piece] = copy
+
+    sent = []
+    arriving = []
+
+    def pass_on(count):
+        for slot, origin in arriving[:count]:
+            block = g_ref.at[origin, twin_part]
+            remote(block, block, twin_send.at[slot], twin_recv.at[slot], twin).wait_recv()
+            copy = remote(block, block, sib_send.at[slot, 2], sib_recv.at[slot, 2], sibling)
+            copy.start()
+            pending.append(copy)
+        del arriving[:count]
 
     for piece in range(pieces):
         send(0, 0, piece)
@@ -99,13 +122,25 @@
                 shift = n - step - 1 if side == 0 else step + 1
                 origin = ring_index((pos + shift) % n, n)
                 slot = side * right_steps + step
-                part = pl.ds(core * half + piece * size, size)
+                part = parts[piece]
+                if paired and piece == 0:
+                    copy = remote(
+                        g_ref.at[origin, part], g_ref.at[origin, part], twin_send.at[slot], twin_recv.at[slot], twin
+                    )
+                    copy.start()
+                    sent.append(copy)
+                    arriving.append((slot, origin))
                 copy = remote(
                     g_ref.at[origin, part], g_ref.at[origin, part],
                     sib_send.at[slot, piece], sib_recv.at[slot, piece], sibling,
                 )
                 copy.start()
                 pending.append(copy)
+        if step:
+            pass_on(2 if step < left_steps + 1 else 1)
+    pass_on(len(arriving))
+    for copy in sent:
+        copy.wait_send()
     for copy in ring.values():
         copy.wait_send()
     for copy in pending + edges:
@@ -113,11 +148,10 @@
     own.wait()
 
 
-def gather(n, w, f, e):
+def gather(n, groups, w, f, e):
     images, _, depth, span = f.shape
-    pieces = 2 if w.shape[0] % 4 == 0 else 1
     return pl.pallas_call(
-        functools.partial(gather_kernel, n, pieces),
+        functools.partial(gather_kernel, n, groups % 2 == 0),
         out_shape=(
             jax.ShapeDtypeStruct((n,) + w.shape, w.dtype),
             jax.ShapeDtypeStruct((2, images, depth, span), f.dtype),
@@ -126,10 +160,12 @@
         in_specs=[pl.BlockSpec(memory_space=pl.ANY)] * 3,
         out_specs=(pl.BlockSpec(memory_space=pl.ANY),) * 3,
         scratch_shapes=[
-            pltpu.SemaphoreType.DMA((n, pieces)),
-            pltpu.SemaphoreType.DMA((n, pieces)),
-            pltpu.SemaphoreType.DMA((n, pieces)),
-            pltpu.SemaphoreType.DMA((n, pieces)),
+            pltpu.SemaphoreType.DMA((n, 2)),
+            pltpu.SemaphoreType.DMA((n, 2)),
+            pltpu.SemaphoreType.DMA((n, 3)),
+            pltpu.SemaphoreType.DMA((n, 3)),
+            pltpu.SemaphoreType.DMA((n,)),
+            pltpu.SemaphoreType.DMA((n,)),
             pltpu.SemaphoreType.DMA((4,)),
             pltpu.SemaphoreType.DMA((4,)),
             pltpu.SemaphoreType.DMA,
@@ -460,6 +496,7 @@
 
 def per_device(
     n,
+    groups,
     latents,
     room_labels,
     timesteps,
@@ -484,7 +521,7 @@
     packed = jnp.concatenate(
         [by_tap(trunk_weight), mix_weight[None], by_tap(control_weight), mix_weight[None]], axis=0
     )
-    gathered, halo, edge = gather(n, packed, columns, edge_out)
+    gathered, halo, edge = gather(n, groups, packed, columns, edge_out)
     if share % 8:
         gathered = gathered.transpose(1, 0, 2, 3).reshape(1, 20, n * share, channels)
     me = lax.axis_index("mp")[None].astype(jnp.int32)
@@ -520,7 +557,7 @@
         P("groups", None),
     )
     return jax.shard_map(
-        functools.partial(per_device, mesh.shape["mp"]),
+        functools.partial(per_device, mesh.shape["mp"], mesh.shape["groups"]),
         mesh=mesh,
         in_specs=in_specs,
         out_specs=out_specs,

time: 168 us -> 164 us (0.976)
  Pallas kernels: 156 us -> 152 us
    pallas_call x1, Pallas kernels: 44.7 us -> 40.4 us  [gather(): pl.pallas_call(functools.partial(gather_kernel, n, groups % 2 == 0), out_...]
where the time goes in v3:
time: 164 us
  Pallas kernels  152 us (93%)
  local copies, waits for them, and re-layouts  7.25 us (4%)
  other arithmetic  3.74 us (2%)
    pallas_call x1, Pallas kernels, compute(): pl.pallas_call(functools.partial(compute_kernel, n, rows, chunks, lanes,...  85.4 us
    pallas_call x1, Pallas kernels, gather(): pl.pallas_call(functools.partial(gather_kernel, n, groups % 2 == 0), out_...  40.4 us
    pallas_call x1, Pallas kernels, reduce(): pl.pallas_call(functools.partial(reduce_kernel, n), out_shape=(jax.ShapeD...  25.8 us

profile of v3, /device:TPU:0, one launch (start us, length us, event | category | flops | bytes accessed | tf_op | source)
XLA Modules:
  0.0 163.6 jit_solution(8063871424723515160)
XLA Ops:
  0.6 0.0 copy-start
  0.7 0.7 convert_element_type.8
  1.4 0.7 slice_bitcast_fusion.2
  2.1 0.2 multiply_cosine_fusion
  2.3 0.0 copy-done
  2.3 0.3 fusion.1
  2.6 0.6 broadcast_in_dim.21.shift_ref
  3.3 0.6 broadcast_in_dim.20.e_ref
  3.9 0.8 pad_maximum_fusion.1
  4.7 0.7 copy.16.tablet_ref
  5.4 2.0 %pad_maximum_fusion.w_ref = bf16[20,40,320]{2,1,0:T(8,128)(2,1)} fusion(bf16[1,40,320]{2,1,0:T(8,128)(2,1)} %bitcast.29, bf16[9,40,320]{2,1,0:T(8,128)(2,1)} %bitcast.27, bf16[9,40,320]{2,1,0:T(8,128)(2,1)} %bitcast.28), kind=kLoop, calls=%fused_computation | loop fusion | flops 768000 | bytes 998400 | tf_op jit(solution)/shard_map/concatenate | solution.py:521
  7.4 40.4 %gather.1 = (bf16[8,20,40,320]{3,2,1,0:T(8,128)(2,1)}, bf16[2,3,320,128]{3,2,1,0:T(8,128)(2,1)}, s32[2,3,8,128]{3,2,1,0:T(8,128)}) custom-call(bf16[20,40,320]{2,1,0:T(8,128)(2,1)} %pad_maximum_fusion.w_ref, bf16[3,16,320,128]{3,2,1,0:T(8,128)(2,1)} %bitcast.22, s32[2,3,8,128]{3,2,1,0:T(8,128)} %broadcast_in_dim.20.e_ref), custom_call_target="tpu_custom_call" | custom-call | tf_op jit(solution)/shard_map/gather/pallas_call | solution.py:153
  47.8 85.4 %convolve.1 = (bf16[3,16,320,128]{3,2,1,0:T(8,128)(2,1)}, bf16[8,10,40,320]{3,2,1,0:T(8,128)(2,1)}, f32[16,320]{1,0:T(8,128)}) custom-call(s32[1]{0:T(128)} %bitcast.me_ref, bf16[3,16,320,128]{3,2,1,0:T(8,128)(2,1)} %bitcast.23, bf16[3,16,320,128]{3,2,1,0:T(8,128)(2,1)} %bitcast.24, bf16[3,16,320,128]{3,2,1,0:T(8,128)(2,1)} %bitcast.25, ...), custom_call_target="tpu_custom_call" | custom-call | flops 60000002048 | bytes 20000000 | tf_op jit(solution)/shard_map/convolve/pallas_call | solution.py:302
  133.2 0.0 copy-start.1
  133.2 1.7 %copy-done.1 = bf16[8,10,40,320]{3,2,1,0:T(8,128)(2,1)S(1)} copy-done((bf16[8,10,40,320]{3,2,1,0:T(8,128)(2,1)S(1)}, bf16[8,10,40,320]{3,2,1,0:T(8,128)(2,1)}, u32[]{:S(2)}) %copy-start.1) | copy-done | bytes 2048024
  134.9 0.0 copy-start.2
  134.9 0.7 copy-done.2
  135.6 25.8 %scatter.1 = (f32[10,40,320]{2,1,0:T(8,128)S(1)}, f32[16,320]{1,0:T(8,128)S(1)}) custom-call(bf16[8,10,40,320]{3,2,1,0:T(8,128)(2,1)S(1)} %copy-done.1, f32[16,320]{1,0:T(8,128)S(1)} %copy-done.2), custom_call_target="tpu_custom_call" | custom-call | flops 1000000000 | bytes 50000000 | tf_op jit(solution)/shard_map/scatter/pallas_call | solution.py:457
  161.5 0.6 slice_bitcast_fusion
  162.1 0.8 slice.14
  163.0 0.6 copy.18
  (4 shorter events, 0.0 us)
Async XLA Ops:
  0.6 1.7 %copy-start = (bf16[1280,320]{0,1:T(8,128)(2,1)S(1)}, bf16[1280,320]{0,1:T(8,128)(2,1)}, u32[]{:S(2)}) copy-start(bf16[1280,320]{0,1:T(8,128)(2,1)} %param.13) | copy-start | bytes 2457604
  133.2 1.7 %copy-start.1 = (bf16[8,10,40,320]{3,2,1,0:T(8,128)(2,1)S(1)}, bf16[8,10,40,320]{3,2,1,0:T(8,128)(2,1)}, u32[]{:S(2)}) copy-start(bf16[8,10,40,320]{3,2,1,0:T(8,128)(2,1)} %get-tuple-element.16.parts_ref) | copy-start | bytes 6144004
  134.9 0.7 copy-start.2
